TPU v7x, 256 devices: a whole 4x4x8 slice. The times are simulated.
256 devices in a mesh: blk: 16 (over x_lo, z), head: 4 (over x_hi, core), rep: 4 (over y).
Axes of the slice: x: 4 (x_hi: 2, x_lo: 2; x = x_hi * 2 + x_lo), y: 4, z: 8, core: 2. Of those that a mesh axis runs over, the one named last changes fastest.
Arguments:
- queries: bfloat16 [8, 256, 8192], P('rep', 'blk', 'head'), parts along dimension 0, may hold values from -16 to 16
- cache_keys: bfloat16 [8, 32768, 8, 128], P('rep', 'blk', 'head'), parts along dimension 0, may hold values from -6 to 6
- cache_values: bfloat16 [8, 32768, 8, 128], P('rep', 'blk', 'head'), parts along dimension 0, may hold values from -6 to 6
- context_lengths: int32 [8], P('rep'), parts along dimension 0, may hold values from 1 to 32512, as said below
- block_order: int32 [8, 16], P('rep'), parts along dimension 0, may hold values from 0 to 15, each once within a row
Outputs:
- attended: bfloat16 [8, 256, 8192], P('rep', 'blk', 'head'), parts along dimension 0
There are 4 independent parts, one for each index of `rep`. A program takes and returns all parts, laid end to end along the dimension named above; each array names one. Nothing has to cross between parts.
Inputs may be any that keep to these rules, and one draw needn't show every extreme that they name: `context_lengths`: in every draw some request has exactly 32512 cached positions. `block_order`: each row is a permutation of the indices along blk.
All inputs are finite; a program needn't handle non-finite values.
Results may differ from a plain program's by a relative error of at most 0.014.
Values may be sent and summed in bfloat16 or wider, within the bound.
A program may use at most 64 MiB of HBM per device.

v0:
```python
import math

import jax
import jax.numpy as jnp
from jax import lax
from jax.sharding import PartitionSpec as P

masked_score = -1e30


def row_positions(context_lengths, block_order, row_count, per_owner):
    row_index = jnp.arange(row_count, dtype=jnp.int32)
    owning = row_index // per_owner
    devices = block_order.shape[1]
    matches = owning[:, None] == jnp.arange(devices, dtype=jnp.int32)[None, :]
    placed = jnp.sum(jnp.where(matches[None, :, :], block_order[:, None, :], 0), axis=2)
    return context_lengths[:, None] + placed * per_owner + (row_index % per_owner)[None, :]


def local_partial(query_rows, positions, cache_keys, cache_values, first_key, initial):
    requests, row_count, width = query_rows.shape
    kv_local = cache_keys.shape[2]
    head_dim = cache_keys.shape[3]
    group_size = width // (kv_local * head_dim)
    grouped = query_rows.reshape(requests, row_count, kv_local, group_size, head_dim)
    span = cache_keys.shape[1]
    block_size = math.gcd(span, 256)
    scaling = head_dim ** (-0.5)

    def update(carry, begin):
        top_now, total_now, summed_now = carry
        key_block = lax.dynamic_slice_in_dim(cache_keys, begin, block_size, 1)
        value_block = lax.dynamic_slice_in_dim(cache_values, begin, block_size, 1)
        key_positions = first_key + begin + jnp.arange(block_size, dtype=jnp.int32)
        visible = key_positions[None, None, None, None, :] <= positions[:, :, None, None, None]
        scores = (
            jnp.einsum("rtkgd,rskd->rtkgs", grouped, key_block, preferred_element_type=jnp.float32)
            * scaling
        )
        scores = jnp.where(visible, scores, masked_score)
        top_next = jnp.maximum(top_now, jnp.max(scores, axis=4))
        weights = jnp.where(visible, jnp.exp(scores - top_next[..., None]), 0.0)
        shrink = jnp.exp(top_now - top_next)
        total_next = total_now * shrink + jnp.sum(weights, axis=4)
        product = jnp.einsum(
            "rtkgs,rskd->rtkgd",
            weights.astype(jnp.bfloat16),
            value_block,
            preferred_element_type=jnp.float32,
        )
        summed_next = summed_now * shrink[..., None] + product
        return (top_next, total_next, summed_next)

    def visit(carry, block_index):
        begin = block_index * block_size
        result = update(carry, begin)
        return (result, None)

    final, ignored = lax.scan(visit, initial, jnp.arange(span // block_size, dtype=jnp.int32))
    return final


def shards(queries, cache_keys, cache_values, context_lengths, block_order):
    requests, per_owner, width = queries.shape
    kv_local = cache_keys.shape[2]
    head_dim = cache_keys.shape[3]
    group_size = width // (kv_local * head_dim)
    my_index = lax.axis_index("blk")
    first_key = my_index * cache_keys.shape[1]
    visiting = lax.all_gather(queries, "blk", axis=1, tiled=True)
    row_count = visiting.shape[1]
    positions = row_positions(context_lengths, block_order, row_count, per_owner)
    state_shape = (requests, row_count, kv_local, group_size)
    partial_value = local_partial(
        visiting,
        positions,
        cache_keys,
        cache_values,
        first_key,
        (
            jnp.full(state_shape, masked_score, jnp.float32),
            jnp.zeros(state_shape, jnp.float32),
            jnp.zeros(state_shape + (head_dim,), jnp.float32),
        ),
    )
    top_all = partial_value[0]
    total_all = partial_value[1]
    summed_all = partial_value[2]
    top_all, total_all, summed_all = (top_all, total_all, summed_all)
    source_tops, source_totals, source_sums = (
        lax.all_to_all(top_all[None], "blk", split_axis=2, concat_axis=0, tiled=True),
        lax.all_to_all(total_all[None], "blk", split_axis=2, concat_axis=0, tiled=True),
        lax.all_to_all(summed_all[None], "blk", split_axis=2, concat_axis=0, tiled=True),
    )
    overall = jnp.max(source_tops, axis=0)
    factor = jnp.exp(source_tops - overall[None])
    denominator = jnp.sum(source_totals * factor, axis=0)
    numerator = jnp.sum(source_sums * factor[..., None], axis=0)
    attended = numerator / denominator[..., None]
    return attended.reshape(requests, per_owner, width).astype(jnp.bfloat16)


def solution(mesh):
    return jax.shard_map(
        shards,
        mesh=mesh,
        in_specs=(
            P("rep", "blk", "head"),
            P("rep", "blk", "head", None),
            P("rep", "blk", "head", None),
            P("rep"),
            P("rep", None),
        ),
        out_specs=P("rep", "blk", "head"),
        check_vma=False,
    )
```

profile of v0, /device:TPU:8, one launch (start us, length us, event | category | flops | bytes accessed | tf_op | source)
XLA Modules:
  0.0 389.6 jit_solution(3073486358533039853)
XLA Ops:
  6.5 1.7 copy.30
  8.3 0.8 select_reduce_fusion
  9.1 0.7 add_add_fusion
  9.8 73.8 %all-gather.2.cloned.1.call-done = bf16[2,256,2048]{2,0,1:T(2,128)(2,1)} async-done(((bf16[2,16,2048]{2,0,1:T(2,128)(2,1)}), bf16[2,256,2048]{2,0,1:T(2,128)(2,1)}) %all-gather.2.cloned.1.call-update) | async-done | bytes 2097168 | tf_op jit(solution)/shard_map/all_gather | solution.py:70
  83.6 6.1 %copy.31 = bf16[2,256,2048]{1,2,0:T(8,128)(2,1)} copy(bf16[2,256,2048]{2,0,1:T(2,128)(2,1)} %all-gather.2.cloned.1.call-done) | data formatting | bytes 4194304 | tf_op jit(solution)/shard_map/all_gather | solution.py:70
  89.7 3.0 copy.33
  92.8 168.7 %while.15 = (s32[]{:T(128)}, f32[2,256,2,8]{1,3,2,0:T(8,128)S(1)}, f32[2,256,2,8]{1,3,2,0:T(8,128)S(1)}, f32[2,256,2,8,128]{1,4,3,2,0:T(8,128)}, s32[8]{0:T(128)...) while((s32[]{:T(128)}, f32[2,256,2,8]{1,3,2,0:T(8,128)S(1)}, ...), condition=%wide.region_4.5_spmd.clone, body=%wide.region_1.4_spmd.clone.sunk | while | flops 1104322816 | bytes 38801628 | solution.py:59
  92.8 0.6 dynamic_slice.18
  94.0 1.4 constant_dynamic-slice_fusion.3
  95.6 4.6 %fusion.33 = (f32[2,256,2,8]{1,3,2,0:T(8,128)S(1)}, f32[2,2,256,256,8]{3,2,4,1,0:T(8,128)}) fusion(pred[2,256,256]{1,2,0:T(8,128)(4,1)S(1)} %broadcast_compare_fusion.2, bf16[2,256,2,8,128]{4,1,3,2,0:T(8,128)(2,1)S(1)} %get-tuple-element.272, bf16[2,256,2,128]{3,2,1,0:T(2,128)(2,1)S(1)} %get-tuple-element.230), kind=kOutput, calls=%fused_computation.2.clone.1 | convolution fusion | flops 543154176 | bytes 10911744 | tf_op jit(solution)/shard_map/while/body/eval_jaxpr/rtkgd,rskd->rtkgs/dot_general | solution.py:37
  100.2 4.5 %fusion.34 = f32[2,256,2,8]{1,3,2,0:T(8,128)S(1)} fusion(f32[2,2,256,256,8]{3,2,4,1,0:T(8,128)} %get-tuple-element.232, f32[2,256,2,8]{1,3,2,0:T(8,128)S(1)} %select_maximum_fusion.2, pred[2,256,256]{1,2,0:T(8,128)(4,1)S(1)} %broadcast_compare_fusion.2), kind=kLoop, calls=%fused_computation.4.clone.1 | loop fusion | flops 10477568 | bytes 8585216 | tf_op jit(solution)/shard_map/while/body/eval_jaxpr/reduce_sum | solution.py:44
  104.9 7.9 %bitcast_add_fusion.2 = f32[2,256,2,8,128]{1,4,3,2,0:T(8,128)} fusion(f32[2,256,2,8,128]{1,4,3,2,0:T(8,128)} %get-tuple-element.253, f32[2,256,2,8]{1,3,2,0:T(8,128)S(1)} %get-tuple-element.234, pred[]{:T(512)S(6)} %compare.8, f32[2,2,256,256,8]{3,2,4,1,0:T(8,128)} %get-tuple-element.232, f32[2,256,2,8]{1,3,2,0:T(8,128)S(1)} %select_maximum_fusion.2, ...), kind=kOutput, calls=%fused_computation.6.clone.1 | convolution fusion | flops 550502400 | bytes 17235968 | tf_op jit(solution)/shard_map/while/body/eval_jaxpr/rtkgs,rskd->rtkgd/dot_general | solution.py:45
  112.8 0.6 dynamic_slice.18
  114.1 1.4 constant_dynamic-slice_fusion.3
  115.6 4.6 %fusion.33 = (f32[2,256,2,8]{1,3,2,0:T(8,128)S(1)}, f32[2,2,256,256,8]{3,2,4,1,0:T(8,128)}) fusion(pred[2,256,256]{1,2,0:T(8,128)(4,1)S(1)} %broadcast_compare_fusion.2, bf16[2,256,2,8,128]{4,1,3,2,0:T(8,128)(2,1)S(1)} %get-tuple-element.272, bf16[2,256,2,128]{3,2,1,0:T(2,128)(2,1)S(1)} %get-tuple-element.230), kind=kOutput, calls=%fused_computation.2.clone.1 | convolution fusion | flops 543154176 | bytes 10911744 | tf_op jit(solution)/shard_map/while/body/eval_jaxpr/rtkgd,rskd->rtkgs/dot_general | solution.py:37
  120.3 4.5 %fusion.34 = f32[2,256,2,8]{1,3,2,0:T(8,128)S(1)} fusion(f32[2,2,256,256,8]{3,2,4,1,0:T(8,128)} %get-tuple-element.232, f32[2,256,2,8]{1,3,2,0:T(8,128)S(1)} %select_maximum_fusion.2, pred[2,256,256]{1,2,0:T(8,128)(4,1)S(1)} %broadcast_compare_fusion.2), kind=kLoop, calls=%fused_computation.4.clone.1 | loop fusion | flops 10477568 | bytes 8585216 | tf_op jit(solution)/shard_map/while/body/eval_jaxpr/reduce_sum | solution.py:44
  125.0 9.1 %bitcast_add_fusion.2 = f32[2,256,2,8,128]{1,4,3,2,0:T(8,128)} fusion(f32[2,256,2,8,128]{1,4,3,2,0:T(8,128)} %get-tuple-element.253, f32[2,256,2,8]{1,3,2,0:T(8,128)S(1)} %get-tuple-element.234, pred[]{:T(512)S(6)} %compare.8, f32[2,2,256,256,8]{3,2,4,1,0:T(8,128)} %get-tuple-element.232, f32[2,256,2,8]{1,3,2,0:T(8,128)S(1)} %select_maximum_fusion.2, ...), kind=kOutput, calls=%fused_computation.6.clone.1 | convolution fusion | flops 550502400 | bytes 17235968 | tf_op jit(solution)/shard_map/while/body/eval_jaxpr/rtkgs,rskd->rtkgd/dot_general | solution.py:45
  134.1 0.6 dynamic_slice.18
  135.3 1.4 constant_dynamic-slice_fusion.3
  136.9 4.6 %fusion.33 = (f32[2,256,2,8]{1,3,2,0:T(8,128)S(1)}, f32[2,2,256,256,8]{3,2,4,1,0:T(8,128)}) fusion(pred[2,256,256]{1,2,0:T(8,128)(4,1)S(1)} %broadcast_compare_fusion.2, bf16[2,256,2,8,128]{4,1,3,2,0:T(8,128)(2,1)S(1)} %get-tuple-element.272, bf16[2,256,2,128]{3,2,1,0:T(2,128)(2,1)S(1)} %get-tuple-element.230), kind=kOutput, calls=%fused_computation.2.clone.1 | convolution fusion | flops 543154176 | bytes 10911744 | tf_op jit(solution)/shard_map/while/body/eval_jaxpr/rtkgd,rskd->rtkgs/dot_general | solution.py:37
  141.5 4.5 %fusion.34 = f32[2,256,2,8]{1,3,2,0:T(8,128)S(1)} fusion(f32[2,2,256,256,8]{3,2,4,1,0:T(8,128)} %get-tuple-element.232, f32[2,256,2,8]{1,3,2,0:T(8,128)S(1)} %select_maximum_fusion.2, pred[2,256,256]{1,2,0:T(8,128)(4,1)S(1)} %broadcast_compare_fusion.2), kind=kLoop, calls=%fused_computation.4.clone.1 | loop fusion | flops 10477568 | bytes 8585216 | tf_op jit(solution)/shard_map/while/body/eval_jaxpr/reduce_sum | solution.py:44
  146.2 9.1 %bitcast_add_fusion.2 = f32[2,256,2,8,128]{1,4,3,2,0:T(8,128)} fusion(f32[2,256,2,8,128]{1,4,3,2,0:T(8,128)} %get-tuple-element.253, f32[2,256,2,8]{1,3,2,0:T(8,128)S(1)} %get-tuple-element.234, pred[]{:T(512)S(6)} %compare.8, f32[2,2,256,256,8]{3,2,4,1,0:T(8,128)} %get-tuple-element.232, f32[2,256,2,8]{1,3,2,0:T(8,128)S(1)} %select_maximum_fusion.2, ...), kind=kOutput, calls=%fused_computation.6.clone.1 | convolution fusion | flops 550502400 | bytes 17235968 | tf_op jit(solution)/shard_map/while/body/eval_jaxpr/rtkgs,rskd->rtkgd/dot_general | solution.py:45
  155.3 0.6 dynamic_slice.18
  156.5 1.4 constant_dynamic-slice_fusion.3
  158.1 4.6 %fusion.33 = (f32[2,256,2,8]{1,3,2,0:T(8,128)S(1)}, f32[2,2,256,256,8]{3,2,4,1,0:T(8,128)}) fusion(pred[2,256,256]{1,2,0:T(8,128)(4,1)S(1)} %broadcast_compare_fusion.2, bf16[2,256,2,8,128]{4,1,3,2,0:T(8,128)(2,1)S(1)} %get-tuple-element.272, bf16[2,256,2,128]{3,2,1,0:T(2,128)(2,1)S(1)} %get-tuple-element.230), kind=kOutput, calls=%fused_computation.2.clone.1 | convolution fusion | flops 543154176 | bytes 10911744 | tf_op jit(solution)/shard_map/while/body/eval_jaxpr/rtkgd,rskd->rtkgs/dot_general | solution.py:37
  162.7 4.5 %fusion.34 = f32[2,256,2,8]{1,3,2,0:T(8,128)S(1)} fusion(f32[2,2,256,256,8]{3,2,4,1,0:T(8,128)} %get-tuple-element.232, f32[2,256,2,8]{1,3,2,0:T(8,128)S(1)} %select_maximum_fusion.2, pred[2,256,256]{1,2,0:T(8,128)(4,1)S(1)} %broadcast_compare_fusion.2), kind=kLoop, calls=%fused_computation.4.clone.1 | loop fusion | flops 10477568 | bytes 8585216 | tf_op jit(solution)/shard_map/while/body/eval_jaxpr/reduce_sum | solution.py:44
  167.4 9.1 %bitcast_add_fusion.2 = f32[2,256,2,8,128]{1,4,3,2,0:T(8,128)} fusion(f32[2,256,2,8,128]{1,4,3,2,0:T(8,128)} %get-tuple-element.253, f32[2,256,2,8]{1,3,2,0:T(8,128)S(1)} %get-tuple-element.234, pred[]{:T(512)S(6)} %compare.8, f32[2,2,256,256,8]{3,2,4,1,0:T(8,128)} %get-tuple-element.232, f32[2,256,2,8]{1,3,2,0:T(8,128)S(1)} %select_maximum_fusion.2, ...), kind=kOutput, calls=%fused_computation.6.clone.1 | convolution fusion | flops 550502400 | bytes 17235968 | tf_op jit(solution)/shard_map/while/body/eval_jaxpr/rtkgs,rskd->rtkgd/dot_general | solution.py:45
  176.5 0.6 dynamic_slice.18
  177.8 1.4 constant_dynamic-slice_fusion.3
  179.3 4.6 %fusion.33 = (f32[2,256,2,8]{1,3,2,0:T(8,128)S(1)}, f32[2,2,256,256,8]{3,2,4,1,0:T(8,128)}) fusion(pred[2,256,256]{1,2,0:T(8,128)(4,1)S(1)} %broadcast_compare_fusion.2, bf16[2,256,2,8,128]{4,1,3,2,0:T(8,128)(2,1)S(1)} %get-tuple-element.272, bf16[2,256,2,128]{3,2,1,0:T(2,128)(2,1)S(1)} %get-tuple-element.230), kind=kOutput, calls=%fused_computation.2.clone.1 | convolution fusion | flops 543154176 | bytes 10911744 | tf_op jit(solution)/shard_map/while/body/eval_jaxpr/rtkgd,rskd->rtkgs/dot_general | solution.py:37
  184.0 4.5 %fusion.34 = f32[2,256,2,8]{1,3,2,0:T(8,128)S(1)} fusion(f32[2,2,256,256,8]{3,2,4,1,0:T(8,128)} %get-tuple-element.232, f32[2,256,2,8]{1,3,2,0:T(8,128)S(1)} %select_maximum_fusion.2, pred[2,256,256]{1,2,0:T(8,128)(4,1)S(1)} %broadcast_compare_fusion.2), kind=kLoop, calls=%fused_computation.4.clone.1 | loop fusion | flops 10477568 | bytes 8585216 | tf_op jit(solution)/shard_map/while/body/eval_jaxpr/reduce_sum | solution.py:44
  188.6 9.1 %bitcast_add_fusion.2 = f32[2,256,2,8,128]{1,4,3,2,0:T(8,128)} fusion(f32[2,256,2,8,128]{1,4,3,2,0:T(8,128)} %get-tuple-element.253, f32[2,256,2,8]{1,3,2,0:T(8,128)S(1)} %get-tuple-element.234, pred[]{:T(512)S(6)} %compare.8, f32[2,2,256,256,8]{3,2,4,1,0:T(8,128)} %get-tuple-element.232, f32[2,256,2,8]{1,3,2,0:T(8,128)S(1)} %select_maximum_fusion.2, ...), kind=kOutput, calls=%fused_computation.6.clone.1 | convolution fusion | flops 550502400 | bytes 17235968 | tf_op jit(solution)/shard_map/while/body/eval_jaxpr/rtkgs,rskd->rtkgd/dot_general | solution.py:45
  197.8 0.6 dynamic_slice.18
  199.0 1.4 constant_dynamic-slice_fusion.3
  200.6 4.6 %fusion.33 = (f32[2,256,2,8]{1,3,2,0:T(8,128)S(1)}, f32[2,2,256,256,8]{3,2,4,1,0:T(8,128)}) fusion(pred[2,256,256]{1,2,0:T(8,128)(4,1)S(1)} %broadcast_compare_fusion.2, bf16[2,256,2,8,128]{4,1,3,2,0:T(8,128)(2,1)S(1)} %get-tuple-element.272, bf16[2,256,2,128]{3,2,1,0:T(2,128)(2,1)S(1)} %get-tuple-element.230), kind=kOutput, calls=%fused_computation.2.clone.1 | convolution fusion | flops 543154176 | bytes 10911744 | tf_op jit(solution)/shard_map/while/body/eval_jaxpr/rtkgd,rskd->rtkgs/dot_general | solution.py:37
  205.2 4.5 %fusion.34 = f32[2,256,2,8]{1,3,2,0:T(8,128)S(1)} fusion(f32[2,2,256,256,8]{3,2,4,1,0:T(8,128)} %get-tuple-element.232, f32[2,256,2,8]{1,3,2,0:T(8,128)S(1)} %select_maximum_fusion.2, pred[2,256,256]{1,2,0:T(8,128)(4,1)S(1)} %broadcast_compare_fusion.2), kind=kLoop, calls=%fused_computation.4.clone.1 | loop fusion | flops 10477568 | bytes 8585216 | tf_op jit(solution)/shard_map/while/body/eval_jaxpr/reduce_sum | solution.py:44
  209.9 9.1 %bitcast_add_fusion.2 = f32[2,256,2,8,128]{1,4,3,2,0:T(8,128)} fusion(f32[2,256,2,8,128]{1,4,3,2,0:T(8,128)} %get-tuple-element.253, f32[2,256,2,8]{1,3,2,0:T(8,128)S(1)} %get-tuple-element.234, pred[]{:T(512)S(6)} %compare.8, f32[2,2,256,256,8]{3,2,4,1,0:T(8,128)} %get-tuple-element.232, f32[2,256,2,8]{1,3,2,0:T(8,128)S(1)} %select_maximum_fusion.2, ...), kind=kOutput, calls=%fused_computation.6.clone.1 | convolution fusion | flops 550502400 | bytes 17235968 | tf_op jit(solution)/shard_map/while/body/eval_jaxpr/rtkgs,rskd->rtkgd/dot_general | solution.py:45
  219.0 0.6 dynamic_slice.18
  220.2 1.4 constant_dynamic-slice_fusion.3
  221.8 4.6 %fusion.33 = (f32[2,256,2,8]{1,3,2,0:T(8,128)S(1)}, f32[2,2,256,256,8]{3,2,4,1,0:T(8,128)}) fusion(pred[2,256,256]{1,2,0:T(8,128)(4,1)S(1)} %broadcast_compare_fusion.2, bf16[2,256,2,8,128]{4,1,3,2,0:T(8,128)(2,1)S(1)} %get-tuple-element.272, bf16[2,256,2,128]{3,2,1,0:T(2,128)(2,1)S(1)} %get-tuple-element.230), kind=kOutput, calls=%fused_computation.2.clone.1 | convolution fusion | flops 543154176 | bytes 10911744 | tf_op jit(solution)/shard_map/while/body/eval_jaxpr/rtkgd,rskd->rtkgs/dot_general | solution.py:37
  226.4 4.5 %fusion.34 = f32[2,256,2,8]{1,3,2,0:T(8,128)S(1)} fusion(f32[2,2,256,256,8]{3,2,4,1,0:T(8,128)} %get-tuple-element.232, f32[2,256,2,8]{1,3,2,0:T(8,128)S(1)} %select_maximum_fusion.2, pred[2,256,256]{1,2,0:T(8,128)(4,1)S(1)} %broadcast_compare_fusion.2), kind=kLoop, calls=%fused_computation.4.clone.1 | loop fusion | flops 10477568 | bytes 8585216 | tf_op jit(solution)/shard_map/while/body/eval_jaxpr/reduce_sum | solution.py:44
  231.1 9.1 %bitcast_add_fusion.2 = f32[2,256,2,8,128]{1,4,3,2,0:T(8,128)} fusion(f32[2,256,2,8,128]{1,4,3,2,0:T(8,128)} %get-tuple-element.253, f32[2,256,2,8]{1,3,2,0:T(8,128)S(1)} %get-tuple-element.234, pred[]{:T(512)S(6)} %compare.8, f32[2,2,256,256,8]{3,2,4,1,0:T(8,128)} %get-tuple-element.232, f32[2,256,2,8]{1,3,2,0:T(8,128)S(1)} %select_maximum_fusion.2, ...), kind=kOutput, calls=%fused_computation.6.clone.1 | convolution fusion | flops 550502400 | bytes 17235968 | tf_op jit(solution)/shard_map/while/body/eval_jaxpr/rtkgs,rskd->rtkgd/dot_general | solution.py:45
  240.2 0.6 dynamic_slice.18
  241.5 1.4 constant_dynamic-slice_fusion.3
  243.0 4.6 %fusion.33 = (f32[2,256,2,8]{1,3,2,0:T(8,128)S(1)}, f32[2,2,256,256,8]{3,2,4,1,0:T(8,128)}) fusion(pred[2,256,256]{1,2,0:T(8,128)(4,1)S(1)} %broadcast_compare_fusion.2, bf16[2,256,2,8,128]{4,1,3,2,0:T(8,128)(2,1)S(1)} %get-tuple-element.272, bf16[2,256,2,128]{3,2,1,0:T(2,128)(2,1)S(1)} %get-tuple-element.230), kind=kOutput, calls=%fused_computation.2.clone.1 | convolution fusion | flops 543154176 | bytes 10911744 | tf_op jit(solution)/shard_map/while/body/eval_jaxpr/rtkgd,rskd->rtkgs/dot_general | solution.py:37
  247.7 4.5 %fusion.34 = f32[2,256,2,8]{1,3,2,0:T(8,128)S(1)} fusion(f32[2,2,256,256,8]{3,2,4,1,0:T(8,128)} %get-tuple-element.232, f32[2,256,2,8]{1,3,2,0:T(8,128)S(1)} %select_maximum_fusion.2, pred[2,256,256]{1,2,0:T(8,128)(4,1)S(1)} %broadcast_compare_fusion.2), kind=kLoop, calls=%fused_computation.4.clone.1 | loop fusion | flops 10477568 | bytes 8585216 | tf_op jit(solution)/shard_map/while/body/eval_jaxpr/reduce_sum | solution.py:44
  252.3 9.1 %bitcast_add_fusion.2 = f32[2,256,2,8,128]{1,4,3,2,0:T(8,128)} fusion(f32[2,256,2,8,128]{1,4,3,2,0:T(8,128)} %get-tuple-element.253, f32[2,256,2,8]{1,3,2,0:T(8,128)S(1)} %get-tuple-element.234, pred[]{:T(512)S(6)} %compare.8, f32[2,2,256,256,8]{3,2,4,1,0:T(8,128)} %get-tuple-element.232, f32[2,256,2,8]{1,3,2,0:T(8,128)S(1)} %select_maximum_fusion.2, ...), kind=kOutput, calls=%fused_computation.6.clone.1 | convolution fusion | flops 550502400 | bytes 17235968 | tf_op jit(solution)/shard_map/while/body/eval_jaxpr/rtkgs,rskd->rtkgd/dot_general | solution.py:45
  262.0 1.4 reshape.77
  263.3 3.9 %all-to-all-start.1 = ((f32[16,1,512]{2,1,0:T(1,128)}), f32[16,1,512]{2,1,0:T(1,128)S(1)}, u32[]{:S(2)}, u32[]{:S(2)}) async-start(f32[16,1,512]{2,1,0:T(1,128)} %reshape.77), calls=%async_computation.1 | async-start | bytes 65536 | tf_op jit(solution)/shard_map/all_to_all | solution.py:91
  267.8 1.4 reshape.79
  269.2 6.6 %all-to-all-done.1 = f32[16,1,512]{2,1,0:T(1,128)S(1)} async-done(((f32[16,1,512]{2,1,0:T(1,128)}), f32[16,1,512]{2,1,0:T(1,128)S(1)}, u32[]{:S(2)}, u32[]{:S(2)}) %all-to-all-start.1) | async-done | bytes 32800 | tf_op jit(solution)/shard_map/all_to_all | solution.py:91
  275.8 3.5 all-to-all-start.2
  279.3 5.5 %copy.35 = f32[2,256,2,8,128]{4,3,2,0,1:T(8,128)} copy(f32[2,256,2,8,128]{1,4,3,2,0:T(8,128)} %get-tuple-element.59) | data formatting | bytes 8388608 | tf_op jit(solution)/shard_map/while | solution.py:59
  284.8 3.1 all-to-all-done.2
  287.9 5.0 %all-to-all-start = ((f32[1,2,256,2,8,128]{5,4,3,1,0,2:T(8,128)}), f32[1,2,256,2,8,128]{5,4,3,1,0,2:T(8,128)}, u32[]{:S(2)}, u32[]{:S(2)}) async-start(f32[1,2,256,2,8,128]{5,4,3,1,0,2:T(8,128)} %bitcast.80), calls=%async_computation | async-start | bytes 8388608 | tf_op jit(solution)/shard_map/all_to_all | solution.py:93
  292.9 0.5 broadcast.124
  293.4 0.7 reduce.2
  294.2 0.8 reshape.78
  295.0 0.7 reduce.1
  295.7 0.8 reshape.80
  297.2 80.8 %all-to-all-done = f32[1,2,256,2,8,128]{5,4,3,1,0,2:T(8,128)} async-done(((f32[1,2,256,2,8,128]{5,4,3,1,0,2:T(8,128)}), f32[1,2,256,2,8,128]{5,4,3,1,0,2:T(8,128)}, u32[]{:S(2)}, u32[]{:S(2)}) %all-to-all-start) | async-done | bytes 4194336 | tf_op jit(solution)/shard_map/all_to_all | solution.py:93
  378.1 2.5 copy.36
  380.6 1.3 multiply_reduce_fusion
  382.0 0.7 convert_element_type.10
  (64 shorter events, 4.4 us)
Async XLA Ops:
  6.5 77.1 %all-gather.2.cloned.1.call-start = ((), (), s32[]{:S(2)}) async-start(), calls=%async_computation.3 | async-start | bytes 2228224 | tf_op jit(solution)/shard_map/all_gather | solution.py:70
  263.3 12.4 %all-to-all-start.1 = ((f32[16,1,512]{2,1,0:T(1,128)}), f32[16,1,512]{2,1,0:T(1,128)S(1)}, u32[]{:S(2)}, u32[]{:S(2)}) async-start(f32[16,1,512]{2,1,0:T(1,128)} %reshape.77), calls=%async_computation.1 | async-start | bytes 65536 | tf_op jit(solution)/shard_map/all_to_all | solution.py:91
  275.8 12.1 %all-to-all-start.2 = ((f32[16,1,512]{2,1,0:T(1,128)}), f32[16,1,512]{2,1,0:T(1,128)S(1)}, u32[]{:S(2)}, u32[]{:S(2)}) async-start(f32[16,1,512]{2,1,0:T(1,128)} %reshape.79), calls=%async_computation.2 | async-start | bytes 65536 | tf_op jit(solution)/shard_map/all_to_all | solution.py:92
  287.9 90.2 %all-to-all-start = ((f32[1,2,256,2,8,128]{5,4,3,1,0,2:T(8,128)}), f32[1,2,256,2,8,128]{5,4,3,1,0,2:T(8,128)}, u32[]{:S(2)}, u32[]{:S(2)}) async-start(f32[1,2,256,2,8,128]{5,4,3,1,0,2:T(8,128)} %bitcast.80), calls=%async_computation | async-start | bytes 8388608 | tf_op jit(solution)/shard_map/all_to_all | solution.py:93
Sparse Core Ops, SparseCore 0:
  9.1 74.4 all-gather.1
where the time goes:
time: 390 us
  waiting for transfers between devices  164 us (42%)
  matrix products  109 us (28%)
  local copies, waits for them, and re-layouts  42.5 us (11%)
  other arithmetic  42.3 us (11%)
  between operations  13.6 us (3%)
  starting transfers between devices  12.4 us (3%)
  loops' own time  5.63 us (1%)
    all_to_all x1, waiting for transfers between devices, shards(): lax.all_to_all(summed_all[None], 'blk', split_axis=2, concat_axis=0, tile...  80.8 us
    all_gather x1, waiting for transfers between devices, shards(): visiting = lax.all_gather(queries, 'blk', axis=1, tiled=True)  73.8 us
    dot_general x8, matrix products, update(): jnp.einsum('rtkgs,rskd->rtkgd', weights.astype(jnp.bfloat16), value_block...  71.7 us
    dot_general x8, matrix products, update(): jnp.einsum('rtkgd,rskd->rtkgs', grouped, key_block, preferred_element_typ...  37.1 us
    reduce_sum x8, other arithmetic, update(): total_next = total_now * shrink + jnp.sum(weights, axis=4)  35.8 us
    dynamic_slice x16, local copies, waits for them, and re-layouts, update(): value_block = lax.dynamic_slice_in_dim(cache_values, begin, block_size, 1)  12.3 us
    unnamed x8, local copies, waits for them, and re-layouts  9.47 us
  transfers between devices with their start and end apart: 4, of which 4 were waited for; matrix products, arithmetic and copies ran while one was open for 3% of the time, Pallas kernels for 0%

commit v1 on v0

v1 whole, which is shorter than its diff:
```python
import functools

import jax
import jax.numpy as jnp
from jax import lax
from jax.experimental import pallas as pl
from jax.experimental.pallas import tpu as pltpu
from jax.sharding import PartitionSpec as P

masked_score = -1e30
lowest_top = -16384.0
MESH = pl.DeviceIdType.MESH
bf16 = jnp.bfloat16
f32 = jnp.float32

slot_column = (0, 1, 0, 0, 1, 1, 0, 0, 0, 0, 1, 1, 0, 1, 1, 1)
slot_offset = (0, 0, 1, -1, 1, -1, 2, -2, 3, -3, 2, -2, 4, 4, 3, -3)


def edge(slot, head):
    table = {
        1: (0, "x"), 2: (0, "up"), 3: (0, "down"), 4: (1, "up"), 5: (1, "down"), 6: (2, "up"), 7: (3, "down"),
        8: (6, "up"), 9: (7, "down"), 10: (6, "x"), 11: (7, "x"), 13: (12, "x"), 14: (8, "x"), 15: (9, "x"),
    }
    if slot == 12:
        return (8, "up") if head == 0 else (9, "down")
    return table[slot]


opposite = {"x": "x", "up": "down", "down": "up"}


def children(slot, head):
    return [b for b in range(1, 16) if edge(b, head)[0] == slot]


def kernel(sizes, q_ref, lengths_ref, order_ref, k_hbm, v_hbm, out_ref,
           qbuf, kraw, vraw, kp, vt, s0, s1, m0, m1, qrel, part, stats, sbuf, rbuf,
           load_sem, gsend, grecv, rsend, rrecv):
    n_z, span, tokens, group_size, dim = sizes
    rows = tokens * group_size
    scaling = dim ** -0.5 * 1.4426950408889634
    me = lax.axis_index("blk")
    column, z = lax.div(me, n_z), lax.rem(me, n_z)
    at = {
        "x": (1 - column) * n_z + z,
        "up": column * n_z + lax.rem(z + 1, n_z),
        "down": column * n_z + lax.rem(z + n_z - 1, n_z),
    }

    loads = []
    for r in range(2):
        for i, (src, dst) in enumerate(((k_hbm, kraw), (v_hbm, vraw))):
            loads.append(pltpu.make_async_copy(src.at[r], dst.at[r], load_sem.at[2 * r + i]))
            loads[-1].start()

    barrier = pltpu.get_barrier_semaphore()
    for name in ("x", "up", "down"):
        pl.semaphore_signal(barrier, inc=1, device_id={"blk": at[name]}, device_id_type=MESH)

    for r in range(2):
        for h in range(2):
            for g in range(group_size):
                begin = (h * group_size + g) * dim
                qbuf[2 * r + h, 0, pl.ds(g * tokens, tokens), :] = q_ref[r, :, pl.ds(begin, dim)]
    pl.semaphore_wait(barrier, 3)

    def gather_copy(rh, slot, head):
        parent, name = edge(slot, head)
        return pltpu.make_async_remote_copy(
            src_ref=qbuf.at[rh, parent], dst_ref=qbuf.at[rh, slot],
            send_sem=gsend.at[rh, slot], recv_sem=grecv.at[rh, slot],
            device_id={"blk": at[opposite[name]]}, device_id_type=MESH)

    def reduce_copy(rh, slot, head):
        parent, name = edge(slot, head)
        return pltpu.make_async_remote_copy(
            src_ref=sbuf.at[rh, slot], dst_ref=rbuf.at[rh, slot],
            send_sem=rsend.at[rh, slot], recv_sem=rrecv.at[rh, slot],
            device_id={"blk": at[name]}, device_id_type=MESH)

    def forward(r, slots):
        for h in range(2):
            rh = 2 * r + h
            for slot in slots:
                if slot:
                    gather_copy(rh, slot, h).wait_recv()
                for child in children(slot, h):
                    gather_copy(rh, child, h).start()

    forward(0, (0,))

    lane_token = lax.rem(lax.broadcasted_iota(jnp.int32, (1, rows), 1), tokens)
    for r in range(2):
        base = lengths_ref[r] - me * span
        for slot in range(16):
            owner_column = column if slot_column[slot] == 0 else 1 - column
            owner = owner_column * n_z + lax.rem(z + slot_offset[slot] + n_z, n_z)
            begin = base + order_ref[r, owner] * tokens
            qrel[4 * r + slot // 4, :, pl.ds(slot % 4 * rows, rows)] = lane_token + begin

    row_index = lax.broadcasted_iota(jnp.int32, (256, 256), 0)
    col_index = lax.broadcasted_iota(jnp.int32, (256, 256), 1)
    source = jnp.where(row_index < 128, 2 * row_index, 2 * row_index - 255)
    pick = jnp.where(col_index == source, 1.0, 0.0).astype(bf16)
    eye = jnp.where(row_index[:dim, :dim] == col_index[:dim, :dim], 1.0, 0.0).astype(bf16)
    ones_rows = jnp.where(lax.broadcasted_iota(jnp.int32, (16, span), 0) == 0, 1.0, 0.0).astype(bf16)

    def split_keys(r):
        def body(j, _):
            block = kraw[r, pl.ds(pl.multiple_of(j * 256, 256), 256), :]
            both = jnp.dot(pick, block, preferred_element_type=f32).astype(bf16)
            for h in range(2):
                kp[2 * r + h, pl.ds(pl.multiple_of(j * 128, 128), 128), :] = both[128 * h : 128 * h + 128]
            return 0
        lax.fori_loop(0, span // 128, body, 0, unroll=4)

    def split_values(r):
        def body(j, _):
            block = vraw[r, pl.ds(pl.multiple_of(j * 256, 256), 256), :]
            both = jnp.dot(pick, block, preferred_element_type=f32).astype(bf16)
            flipped = lax.dot_general(eye, both, (((1,), (1,)), ((), ())), preferred_element_type=f32).astype(bf16)
            for h in range(2):
                vt[2 * r + h, pl.ds(0, dim), pl.ds(pl.multiple_of(j * 128, 128), 128)] = flipped[:, 128 * h : 128 * h + 128]
            return 0
        lax.fori_loop(0, span // 128, body, 0, unroll=4)
        for h in range(2):
            vt[2 * r + h, pl.ds(dim, 16), :] = ones_rows

    def tile(t):
        r, step, h = lax.div(t, 8), lax.div(lax.rem(t, 8), 2), lax.rem(t, 2)
        return r, jnp.where(r == 0, step, 3 - step), h

    chunk = 256

    def half(following, current, s_next, m_next, s_now, m_now):
        if following is not None:
            r, g, h = tile(following)
            key_at = 2 * r + h
            q = qbuf[key_at, pl.ds(g * 4, 4)].reshape(4 * rows, dim)
            limit = qrel[4 * r + g]
            top = None
        if current is not None:
            rc, gc, hc = tile(current)
            now_at = 2 * rc + hc
            top_now = m_now[...]
            total = None
        for j in range(span // chunk):
            where = pl.ds(j * chunk, chunk)
            if following is not None:
                s = lax.dot_general(kp[key_at, where, :], q, (((1,), (1,)), ((), ())), preferred_element_type=f32)
                index = lax.broadcasted_iota(jnp.int32, (chunk, 1), 0) + j * chunk
                s = jnp.where(index <= limit, s * scaling, masked_score)
                s_next[where, :] = s
                high = jnp.max(s, axis=0, keepdims=True)
                top = high if top is None else jnp.maximum(top, high)
            if current is not None:
                w = jnp.exp2(s_now[where, :] - top_now).astype(bf16)
                x = jnp.dot(vt[now_at, :, where], w, preferred_element_type=f32)
                total = x if total is None else total + x
        if following is not None:
            m_next[...] = jnp.ceil(jnp.maximum(top, lowest_top))
        if current is not None:
            for i in range(4):
                cut = slice(i * rows, i * rows + rows)
                o = total[:dim, cut]
                top_i, sum_i = top_now[:, cut], total[dim : dim + 1, cut]
                part[now_at, gc * 4 + i] = o
                stats[now_at, gc * 4 + i] = jnp.concatenate([top_i, sum_i], axis=0)
                put(now_at, gc * 4 + i, o, top_i, sum_i)

    def put(rh, slot, o, top, total):
        sbuf[rh, slot, pl.ds(0, dim), :] = o.astype(bf16)
        row = lax.broadcasted_iota(jnp.int32, (16, rows), 0)
        top_hi = top.astype(bf16).astype(f32)
        total_hi = total.astype(bf16).astype(f32)
        tail = jnp.where(row == 0, top_hi, jnp.where(row == 1, top - top_hi, jnp.where(row == 2, total_hi, total - total_hi)))
        sbuf[rh, slot, pl.ds(dim, 16), :] = tail.astype(bf16)

    def merged(rh, slot, head):
        own = stats[rh, slot]
        tops, totals, sums = [own[0:1]], [own[1:2]], [part[rh, slot]]
        for child in children(slot, head):
            reduce_copy(rh, child, head).wait_recv()
            tail = rbuf[rh, child, pl.ds(dim, 16), :].astype(f32)
            tops.append(tail[0:1] + tail[1:2])
            totals.append(tail[2:3] + tail[3:4])
            sums.append(rbuf[rh, child, pl.ds(0, dim), :].astype(f32))
        top = functools.reduce(jnp.maximum, tops)
        factors = [jnp.exp2(x - top) for x in tops]
        total = sum(f * x for f, x in zip(factors, totals))
        o = sum(f * x for f, x in zip(factors, sums))
        return o, top, total

    def pass_on(r, slots):
        for h in range(2):
            for slot in slots:
                put(2 * r + h, slot, *merged(2 * r + h, slot, h))
                reduce_copy(2 * r + h, slot, h).start()

    def finish(r):
        for h in range(2):
            o, top, total = merged(2 * r + h, 0, h)
            result = (o / total).T.astype(bf16)
            for g in range(group_size):
                out_ref[r, :, pl.ds((h * group_size + g) * dim, dim)] = result[g * tokens : (g + 1) * tokens]

    leaves = {1: (4, 5), 2: (10, 11), 3: (13, 14, 15)}

    def send_leaves(t):
        r, g, h = tile(t)
        for group, slots in leaves.items():
            @pl.when(g == group)
            def _():
                for slot in slots:
                    reduce_copy(2 * r + h, slot, 0).start()

    def wait_gathered(r, slots):
        for h in range(2):
            for slot in slots:
                gather_copy(2 * r + h, slot, h).wait_recv()

    def after(t, static=None):
        plan = {
            0: lambda: (forward(0, (8, 9)), wait_gathered(0, (4, 5)), forward(1, (1, 2, 3))),
            1: lambda: (loads[2].wait(), split_keys(1)),
            2: lambda: (forward(0, (12,)), wait_gathered(0, (10, 11)), forward(1, (6, 7))),
            3: lambda: (loads[3].wait(), split_values(1)),
            4: lambda: (wait_gathered(0, (13, 14, 15)), forward(1, (8, 9))),
            5: lambda: (forward(1, (12,)),),
            6: lambda: (wait_gathered(1, (4, 5, 10, 11, 13, 14, 15)),),
            8: lambda: pass_on(0, (12,)),
            9: lambda: pass_on(0, (8, 9)),
            10: lambda: pass_on(0, (6, 7)),
            11: lambda: (pass_on(0, (2, 3, 1)), pass_on(1, (12,))),
            12: lambda: (pass_on(1, (8, 9)),),
            13: lambda: (finish(0), pass_on(1, (6, 7))),
        }
        if static is not None:
            if static in plan:
                plan[static]()
            return
        for when, action in plan.items():
            pl.when(t == when)(action_of(action))

    def action_of(action):
        def run():
            action()
        return run

    loads[0].wait()
    split_keys(0)
    forward(0, (1, 2, 3))
    forward(1, (0,))
    loads[1].wait()
    split_values(0)
    forward(0, (6, 7))
    half(0, None, s0, m0, None, None)

    def pair(i, _):
        t = 2 * i
        half(t + 1, t, s1, m1, s0, m0)
        send_leaves(t)
        after(t)
        half(t + 2, t + 1, s0, m0, s1, m1)
        send_leaves(t + 1)
        after(t + 1)
        return 0

    lax.fori_loop(0, 7, pair, 0)
    half(15, 14, s1, m1, s0, m0)
    half(None, 15, None, None, s1, m1)
    pass_on(1, (2, 3, 1))
    finish(1)

    def drain(slot, _):
        for rh in range(4):
            pltpu.make_async_remote_copy(
                src_ref=qbuf.at[rh, slot], dst_ref=qbuf.at[rh, slot], send_sem=gsend.at[rh, slot],
                recv_sem=grecv.at[rh, slot], device_id={"blk": at["x"]}, device_id_type=MESH).wait_send()
            pltpu.make_async_remote_copy(
                src_ref=sbuf.at[rh, slot], dst_ref=rbuf.at[rh, slot], send_sem=rsend.at[rh, slot],
                recv_sem=rrecv.at[rh, slot], device_id={"blk": at["x"]}, device_id_type=MESH).wait_send()
        return 0

    lax.fori_loop(1, 16, drain, 0)


def shards(n_blk, queries, cache_keys, cache_values, context_lengths, block_order):
    requests, tokens, width = queries.shape
    span, kv_local, dim = cache_keys.shape[1:]
    group_size = width // (kv_local * dim)
    rows = tokens * group_size
    n_z = n_blk // 2
    vmem = pl.BlockSpec(memory_space=pltpu.VMEM)
    smem = pl.BlockSpec(memory_space=pltpu.SMEM)
    hbm = pl.BlockSpec(memory_space=pl.ANY)
    keys = cache_keys.reshape(requests, span * kv_local, dim)
    values = cache_values.reshape(requests, span * kv_local, dim)
    pairs = requests * kv_local
    return pl.pallas_call(
        functools.partial(kernel, (n_z, span, tokens, group_size, dim)),
        out_shape=jax.ShapeDtypeStruct(queries.shape, bf16),
        in_specs=[vmem, smem, smem, hbm, hbm],
        out_specs=vmem,
        scratch_shapes=[
            pltpu.VMEM((pairs, 16, rows, dim), bf16),
            pltpu.VMEM((requests, span * kv_local, dim), bf16),
            pltpu.VMEM((requests, span * kv_local, dim), bf16),
            pltpu.VMEM((pairs, span, dim), bf16),
            pltpu.VMEM((pairs, dim + 16, span), bf16),
            pltpu.VMEM((span, 4 * rows), f32),
            pltpu.VMEM((span, 4 * rows), f32),
            pltpu.VMEM((1, 4 * rows), f32),
            pltpu.VMEM((1, 4 * rows), f32),
            pltpu.VMEM((requests * 4, 1, 4 * rows), jnp.int32),
            pltpu.VMEM((pairs, 16, dim, rows), f32),
            pltpu.VMEM((pairs, 16, 2, rows), f32),
            pltpu.VMEM((pairs, 16, dim + 16, rows), bf16),
            pltpu.VMEM((pairs, 16, dim + 16, rows), bf16),
            pltpu.SemaphoreType.DMA((4,)),
            pltpu.SemaphoreType.DMA((pairs, 16)),
            pltpu.SemaphoreType.DMA((pairs, 16)),
            pltpu.SemaphoreType.DMA((pairs, 16)),
            pltpu.SemaphoreType.DMA((pairs, 16)),
        ],
        compiler_params=pltpu.CompilerParams(
            collective_id=0, has_side_effects=True, vmem_limit_bytes=62 << 20
        ),
    )(queries, context_lengths, block_order, keys, values)


def solution(mesh):
    return jax.shard_map(
        functools.partial(shards, mesh.shape["blk"]),
        mesh=mesh,
        in_specs=(
            P("rep", "blk", "head"),
            P("rep", "blk", "head", None),
            P("rep", "blk", "head", None),
            P("rep"),
            P("rep", None),
        ),
        out_specs=P("rep", "blk", "head"),
        check_vma=False,
    )
```

time: 390 us -> 75.2 us (0.19)
  waiting for transfers between devices: 164 us -> 0 us
  matrix products: 109 us -> 0 us
  Pallas kernels: 0 us -> 73.1 us
  other arithmetic: 42.3 us -> 0 us
  local copies, waits for them, and re-layouts: 42.5 us -> 1.57 us
  between operations: 13.6 us -> 0.01 us
  starting transfers between devices: 12.4 us -> 0 us
  loops' own time: 5.63 us -> 0 us
    dot_general x16 -> x0, matrix products: 109 us -> none  [the longest x8 71.7 us: update(): jnp.einsum('rtkgs,rskd->rtkgd', weights.astype(jnp.bfloat16), value_block...]
    all_to_all x3 -> x0, waiting for transfers between devices: 90.6 us -> none  [the longest x1 80.8 us: shards(): lax.all_to_all(summed_all[None], 'blk', split_axis=2, concat_axis=0, tile...]
    all_gather x1 -> x0, waiting for transfers between devices: 73.8 us -> none  [shards(): visiting = lax.all_gather(queries, 'blk', axis=1, tiled=True)]
    pallas_call x0 -> x1, Pallas kernels: none -> 73.1 us  [shards(): pl.pallas_call(functools.partial(kernel, (n_z, span, tokens, group_size,...]
    reduce_sum x11 -> x0, other arithmetic: 38.4 us -> none  [the longest x8 35.8 us: update(): total_next = total_now * shrink + jnp.sum(weights, axis=4)]
    dynamic_slice x24 -> x0, local copies, waits for them, and re-layouts: 17 us -> none  [the longest x16 12.3 us: update(): value_block = lax.dynamic_slice_in_dim(cache_values, begin, block_size, 1)]
    all_to_all x3 -> x0, starting transfers between devices: 12.4 us -> none  [the longest x1 5 us: shards(): lax.all_to_all(summed_all[None], 'blk', split_axis=2, concat_axis=0, tile...]
    unnamed x8 -> x1, local copies, waits for them, and re-layouts: 9.47 us -> 1.57 us
  transfers between devices with their start and end apart: 4 -> 0, of which waited for: 4 -> 0; matrix products, arithmetic and copies ran while one was open for 3% -> 0% of each run, Pallas kernels for 0% -> 0%
where the time goes in v1:
time: 75.2 us; the launch traced here: 74.7 us
  Pallas kernels  73.1 us (97%)
  local copies, waits for them, and re-layouts  1.57 us (2%)
    pallas_call x1, Pallas kernels, shards(): pl.pallas_call(functools.partial(kernel, (n_z, span, tokens, group_size,...  73.1 us
    unnamed x1, local copies, waits for them, and re-layouts  1.57 us

profile of v1, /device:TPU:8, one launch (start us, length us, event | category | flops | bytes accessed | tf_op | source)
XLA Modules:
  0.0 74.7 jit_solution(6514809851837065894)
XLA Ops:
  0.0 73.1 %shard_map.55 = bf16[2,16,2048]{2,1,0:T(8,128)(2,1)} custom-call(bf16[2,16,2048]{2,1,0:T(8,128)(2,1)} %q_ref.1, s32[2]{0:T(128)} %lengths_ref.1, s32[2,16]{1,0:T(2,128)} %order_ref.1, bf16[2,4096,128]{2,1,0:T(8,128)(2,1)} %bitcast.2, bf16[2,4096,128]{2,1,0:T(8,128)(2,1)} %bitcast.3), custom_call_target="tpu_custom_call" | custom-call | tf_op jit(solution)/shard_map/pallas_call | solution.py:301
  73.1 1.6 %copy.7 = bf16[2,16,2048]{2,1,0:T(8,128)(2,1)} copy(bf16[2,16,2048]{2,1,0:T(8,128)(2,1)} %shard_map.55) | data formatting | bytes 262144

commit v2 on v1

v2 whole, which is shorter than its diff:
```python
import functools

import jax
import jax.numpy as jnp
from jax import lax
from jax.experimental import pallas as pl
from jax.experimental.pallas import tpu as pltpu
from jax.sharding import PartitionSpec as P

masked_score = -1e30
lowest_top = -16384.0
MESH = pl.DeviceIdType.MESH
bf16 = jnp.bfloat16
f32 = jnp.float32

slot_column = (0, 1, 0, 0, 1, 1, 0, 0, 0, 0, 1, 1, 0, 1, 1, 1)
slot_offset = (0, 0, 1, -1, 1, -1, 2, -2, 3, -3, 2, -2, 4, 4, 3, -3)

gather_trees = ("Q", "T2")
reduce_trees = ("T2", "Q")
groups = ((5, 12, 15, 7), (11, 8, 9, 10), (4, 13, 14, 3), (6, 0, 2, 1))
tile_order = ((0, 3), (0, 1), (1, 3), (0, 0), (0, 2), (1, 1), (1, 0), (2, 3), (1, 2), (2, 0), (3, 3), (2, 2), (3, 0), (3, 2), (2, 1), (3, 1))
plan = {
    "keys": [("f", 0, 0), ("f", 1, 0)],
    "values": [],
    "first": [("f", 0, 1), ("f", 0, 6), ("f", 0, 7), ("f", 1, 1), ("w", 0, 2)],
    0: [("f", 2, 0), ("f", 3, 0), ("f", 1, 6), ("f", 1, 7), ("f", 0, 8), ("f", 0, 9), ("w", 0, 11), ("w", 0, 10)],
    1: [("f", 0, 12), ("f", 2, 1), ("f", 2, 3), ("f", 3, 1), ("f", 3, 3), ("w", 1, 2)],
    2: [("f", 1, 9), ("f", 2, 2), ("r", 0, 11), ("r", 0, 10), ("f", 3, 2), ("w", 0, 5), ("w", 0, 15)],
    3: [("f", 1, 8), ("f", 1, 12), ("w", 0, 4), ("w", 0, 13), ("w", 0, 14), ("w", 0, 3)],
    4: [("f", 2, 4), ("f", 2, 7), ("r", 0, 15), ("r", 0, 5), ("w", 1, 11), ("w", 1, 10)],
    5: [("f", 2, 6), ("r", 0, 14), ("r", 0, 13), ("f", 3, 5), ("f", 3, 6), ("f", 3, 7), ("r", 0, 4), ("w", 1, 5), ("w", 1, 15)],
    6: [("f", 2, 9), ("r", 1, 11), ("r", 1, 10)],
    7: [("f", 2, 8), ("r", 0, 9), ("r", 0, 8), ("r", 1, 15), ("w", 1, 4), ("w", 1, 13), ("w", 1, 14), ("w", 1, 3)],
    8: [("f", 2, 12), ("r", 0, 12), ("f", 3, 9), ("f", 3, 8), ("r", 2, 2), ("f", 3, 12), ("w", 2, 5), ("w", 2, 15)],
    9: [("r", 0, 1), ("r", 1, 14), ("r", 1, 13), ("r", 1, 5), ("r", 1, 4), ("r", 0, 7)],
    10: [("r", 1, 9), ("r", 2, 15), ("r", 2, 5), ("w", 2, 13), ("w", 2, 14)],
    11: [("r", 0, 6), ("r", 3, 2), ("w", 3, 15)],
    12: [("r", 0, 3), ("r", 1, 1), ("r", 2, 14), ("r", 2, 13), ("r", 2, 4), ("r", 2, 3), ("w", 3, 4), ("w", 3, 13), ("w", 3, 14)],
    13: [("r", 1, 8), ("r", 3, 15), ("r", 3, 5), ("w", 2, 11), ("w", 2, 10)],
    14: [("r", 0, 2), ("r", 1, 12), ("r", 3, 14), ("r", 3, 13), ("r", 3, 4), ("r", 3, 3), ("w", 3, 11), ("w", 3, 10)],
    15: [("r", 2, 11), ("r", 2, 10), ("r", 2, 9), ("r", 2, 8), ("r", 2, 1)],
    "last": [("r", 1, 6), ("r", 2, 12), ("r", 3, 11), ("r", 3, 10), ("r", 3, 9), ("r", 0, 0), ("r", 3, 8), ("r", 3, 1), ("r", 1, 7), ("r", 3, 12), ("r", 1, 2), ("r", 2, 7), ("r", 2, 6), ("r", 1, 3), ("r", 3, 6), ("r", 3, 7), ("r", 2, 0), ("r", 1, 0), ("r", 3, 0)],
}
split_steps = (1, 6)


def edge(tree, slot, head):
    table = {
        1: (0, "x"), 2: (0, "up"), 3: (0, "down"), 4: (1, "up"), 5: (1, "down"), 6: (2, "up"), 7: (3, "down"),
        8: (6, "up"), 9: (7, "down"), 10: (6, "x"), 11: (7, "x"), 13: (12, "x"), 14: (8, "x"), 15: (9, "x"),
        12: (6, "up2") if head == 0 else (7, "down2"),
    }
    if tree == "Q":
        table.update({6: (0, "up2"), 7: (0, "down2")})
    if tree in ("M", "M2"):
        table[12] = (8, "up") if head == 0 else (9, "down")
    if tree in ("M2", "T2"):
        table.update({10: (4, "up")} if head == 0 else {11: (5, "down")})
    return table[slot]


opposite = {"x": "x", "up": "down", "down": "up", "up2": "down2", "down2": "up2"}
place = {slot: 4 * g + i for g, slots in enumerate(groups) for i, slot in enumerate(slots)}


def children(tree, slot, head):
    return [b for b in range(1, 16) if edge(tree, b, head)[0] == slot]


def packed(values):
    return functools.reduce(lambda total, iv: total | (iv[1] << (2 * iv[0])), enumerate(values), 0)


def signed(value):
    return value - (1 << 32) if value >= 1 << 31 else value


pair_code = signed(packed([rh for rh, g in tile_order]))
group_code = signed(packed([g for rh, g in tile_order]))


def kernel(sizes, q_ref, lengths_ref, order_ref, k_hbm, v_hbm, out_ref,
           qbuf, kraw0, kraw1, vraw0, vraw1, kp, vt, s0, s1, m0, m1, qrel, part, stats, sbuf, rbuf,
           load_sem, gsend, grecv, rsend, rrecv):
    n_z, span, tokens, group_size, dim = sizes
    rows = tokens * group_size
    chunk = 256
    chunks = span // chunk
    assert chunks == 8
    scaling = dim ** -0.5 * 1.4426950408889634
    me = lax.axis_index("blk")
    column, z = lax.div(me, n_z), lax.rem(me, n_z)
    at = {
        "x": (1 - column) * n_z + z,
        "up": column * n_z + lax.rem(z + 1, n_z),
        "down": column * n_z + lax.rem(z + n_z - 1, n_z),
        "up2": column * n_z + lax.rem(z + 2, n_z),
        "down2": column * n_z + lax.rem(z + n_z - 2, n_z),
    }
    kraw, vraw = (kraw0, kraw1), (vraw0, vraw1)

    loads = []
    for r in range(2):
        for i, (src, dst) in enumerate(((k_hbm, kraw), (v_hbm, vraw))):
            loads.append(pltpu.make_async_copy(src.at[r], dst[r], load_sem.at[2 * r + i]))
            loads[-1].start()

    barrier = pltpu.get_barrier_semaphore()
    for name in at:
        pl.semaphore_signal(barrier, inc=1, device_id={"blk": at[name]}, device_id_type=MESH)

    for r in range(2):
        for h in range(2):
            for g in range(group_size):
                begin = (h * group_size + g) * dim
                qbuf[2 * r + h, place[0], pl.ds(g * tokens, tokens), :] = q_ref[r, :, pl.ds(begin, dim)]
    pl.semaphore_wait(barrier, len(at))

    def gather_copy(rh, slot):
        parent, name = edge(gather_trees[rh // 2], slot, rh % 2)
        return pltpu.make_async_remote_copy(
            src_ref=qbuf.at[rh, place[parent]], dst_ref=qbuf.at[rh, place[slot]],
            send_sem=gsend.at[rh, slot], recv_sem=grecv.at[rh, slot],
            device_id={"blk": at[opposite[name]]}, device_id_type=MESH)

    def reduce_copy(rh, slot):
        parent, name = edge(reduce_trees[rh // 2], slot, rh % 2)
        return pltpu.make_async_remote_copy(
            src_ref=sbuf.at[rh, place[slot]], dst_ref=rbuf.at[rh, slot],
            send_sem=rsend.at[rh, slot], recv_sem=rrecv.at[rh, slot],
            device_id={"blk": at[name]}, device_id_type=MESH)

    def forward(rh, slot):
        tree = gather_trees[rh // 2]
        if slot:
            gather_copy(rh, slot).wait_recv()
        for child in sorted(children(tree, slot, rh % 2), key=lambda b: -len(children(tree, b, rh % 2))):
            gather_copy(rh, child).start()

    first, limits = [], []
    lane_token = lax.rem(lax.broadcasted_iota(jnp.int32, (1, rows), 1), tokens)

    def set_positions():
        for r in range(2):
            base = lengths_ref[r] - me * span
            first.append(lax.div(jnp.clip(base, 0, span - 2 * chunk), chunk))
            limits.append(base + n_z * 2 * tokens)
            for slot in range(16):
                owner_column = column if slot_column[slot] == 0 else 1 - column
                owner = owner_column * n_z + lax.rem(z + slot_offset[slot] + n_z, n_z)
                begin = base + order_ref[r, owner] * tokens - first[r] * chunk
                qrel[4 * r + place[slot] // 4, :, pl.ds(place[slot] % 4 * rows, rows)] = lane_token + begin

    row_index = lax.broadcasted_iota(jnp.int32, (256, 256), 0)
    col_index = lax.broadcasted_iota(jnp.int32, (256, 256), 1)
    source = jnp.where(row_index < 128, 2 * row_index, 2 * row_index - 255)
    pick = jnp.where(col_index == source, 1.0, 0.0).astype(bf16)
    eye = jnp.where(row_index[:dim, :dim] == col_index[:dim, :dim], 1.0, 0.0).astype(bf16)
    sub_row = lax.broadcasted_iota(jnp.int32, (128, 1), 0)

    def rotate(r, raw):
        bits = [first[r] >> i & 1 for i in range(3)]

        def body(i, _):
            places = [pl.ds(pl.multiple_of(b * 512 + i * 64, 64), 64) for b in range(chunks)]
            blocks = [raw[p, :] for p in places]
            for level, bit in enumerate(bits):
                blocks = [jnp.where(bit == 1, blocks[(b + (1 << level)) % chunks], blocks[b]) for b in range(chunks)]
            for p, block in zip(places, blocks):
                raw[p, :] = block
            return 0

        lax.fori_loop(0, 8, body, 0)

    def split_blocks(r, raw, j):
        pieces, begins = [], []
        for i in range(4):
            block = lax.rem(first[r] + j + i // 2, chunks)
            pieces.append(raw[pl.ds(j * 512 + i * 256, 256), :])
            begins.append(block * chunk + (i % 2) * 128)
        both = jnp.dot(pick, jnp.concatenate(pieces, axis=1), preferred_element_type=f32)
        return [[both[128 * h : 128 * h + 128, 128 * i : 128 * i + 128] for i in range(4)] for h in range(2)], begins

    def split_keys(r):
        head_rows = kraw[r][pl.ds(0, 16), :].astype(f32)
        rotate(r, kraw[r])
        for j in range(0, chunks, 2):
            both, begins = split_blocks(r, kraw[r], j)
            for h in range(2):
                for i in range(4):
                    seen = sub_row + begins[i] < limits[r]
                    kp[2 * r + h, pl.ds(j * chunk + i * 128, 128), :] = jnp.where(seen, both[h][i], head_rows[h : h + 1]).astype(bf16)

    def split_values(r):
        rotate(r, vraw[r])
        for j in range(0, chunks, 2):
            both, begins = split_blocks(r, vraw[r], j)
            kept = [jnp.where(sub_row + begins[i] < limits[r], both[h][i], 0.0).astype(bf16) for h in range(2) for i in range(4)]
            flipped = lax.dot_general(eye, jnp.concatenate(kept, axis=0), (((1,), (1,)), ((), ())), preferred_element_type=f32).astype(bf16)
            for h in range(2):
                vt[2 * r + h, pl.ds(0, dim), pl.ds(j * chunk, 512)] = flipped[:, 512 * h : 512 * h + 512]
            row = lax.broadcasted_iota(jnp.int32, (16, 128), 0)
            lane = lax.broadcasted_iota(jnp.int32, (16, 128), 1)
            for i in range(4):
                counted = jnp.where((row == 0) & (lane + begins[i] < limits[r]), 1.0, 0.0).astype(bf16)
                for h in range(2):
                    vt[2 * r + h, pl.ds(dim, 16), pl.ds(j * chunk + i * 128, 128)] = counted

    def tile(t):
        t = jnp.int32(t)
        rh = jnp.int32(pair_code) >> (2 * t) & 3
        return rh, jnp.int32(group_code) >> (2 * t) & 3

    def half(following, current, s_next, m_next, s_now, m_now):
        if following is not None:
            key_at, g = tile(following)
            q = qbuf[key_at, pl.ds(g * 4, 4)].reshape(4 * rows, dim)
            limit = qrel[4 * (key_at >> 1) + g]
            top = None
        if current is not None:
            now_at, gc = tile(current)
            top_now = m_now[...]
            total = None
        for j in range(chunks):
            where = pl.ds(j * chunk, chunk)
            if following is not None:
                s = lax.dot_general(kp[key_at, where, :], q, (((1,), (1,)), ((), ())), preferred_element_type=f32) * scaling
                if j < 2:
                    index = lax.broadcasted_iota(jnp.int32, (chunk, 1), 0) + j * chunk
                    s = jnp.where(index <= limit, s, masked_score)
                s_next[where, :] = s
                high = jnp.max(s, axis=0, keepdims=True)
                top = high if top is None else jnp.maximum(top, high)
            if current is not None:
                w = jnp.exp2(s_now[where, :] - top_now).astype(bf16)
                x = jnp.dot(vt[now_at, :, where], w, preferred_element_type=f32)
                total = x if total is None else total + x
        if following is not None:
            m_next[...] = jnp.ceil(jnp.maximum(top, lowest_top))
        if current is not None:
            for i in range(4):
                cut = slice(i * rows, i * rows + rows)
                o, sum_i = total[:dim, cut], total[dim : dim + 1, cut]
                top_i = jnp.where(sum_i > 0.0, top_now[:, cut], lowest_top)
                part[now_at, gc * 4 + i] = o
                stats[now_at, gc * 4 + i] = jnp.concatenate([top_i, sum_i], axis=0)
                put(now_at, gc * 4 + i, o, top_i, sum_i)

    def put(rh, spot, o, top, total):
        sbuf[rh, spot, pl.ds(0, dim), :] = o.astype(bf16)
        row = lax.broadcasted_iota(jnp.int32, (16, rows), 0)
        top_hi = top.astype(bf16).astype(f32)
        total_hi = total.astype(bf16).astype(f32)
        tail = jnp.where(row == 0, top_hi, jnp.where(row == 1, top - top_hi, jnp.where(row == 2, total_hi, total - total_hi)))
        sbuf[rh, spot, pl.ds(dim, 16), :] = tail.astype(bf16)

    def merged(rh, slot, kids):
        own = stats[rh, place[slot]]
        tops, totals, sums = [own[0:1]], [own[1:2]], [part[rh, place[slot]]]
        for child in kids:
            reduce_copy(rh, child).wait_recv()
            tail = rbuf[rh, child, pl.ds(dim, 16), :].astype(f32)
            tops.append(tail[0:1] + tail[1:2])
            totals.append(tail[2:3] + tail[3:4])
            sums.append(rbuf[rh, child, pl.ds(0, dim), :].astype(f32))
        top = functools.reduce(jnp.maximum, tops)
        factors = [jnp.exp2(x - top) for x in tops]
        total = sum(f * x for f, x in zip(factors, totals))
        o = sum(f * x for f, x in zip(factors, sums))
        return o, top, total

    def send_back(rh, slot):
        kids = children(reduce_trees[rh // 2], slot, rh % 2)
        if slot:
            if kids:
                put(rh, place[slot], *merged(rh, slot, kids))
            reduce_copy(rh, slot).start()
            return
        o, top, total = merged(rh, slot, kids)
        result = (o / total).T.astype(bf16)
        for g in range(group_size):
            begin = (rh % 2 * group_size + g) * dim
            out_ref[rh // 2, :, pl.ds(begin, dim)] = result[g * tokens : (g + 1) * tokens]

    def act(step):
        if step in split_steps:
            i = split_steps.index(step)
            loads[2 + i].wait()
            (split_keys, split_values)[i](1)
        for kind, rh, slot in plan[step]:
            if kind == "w":
                gather_copy(rh, slot).wait_recv()
            elif kind == "f":
                forward(rh, slot)
            else:
                send_back(rh, slot)

    def act_at(t, steps):
        for step in steps:
            if plan[step] or step in split_steps:
                @pl.when(t == step)
                def _():
                    act(step)

    act("keys")
    set_positions()
    loads[0].wait()
    split_keys(0)
    act("values")
    loads[1].wait()
    split_values(0)
    act("first")
    half(0, None, s0, m0, None, None)

    def pair(i, _):
        t = 2 * i
        act_at(t, range(0, 14, 2))
        half(t + 1, t, s1, m1, s0, m0)
        act_at(t + 1, range(1, 14, 2))
        half(t + 2, t + 1, s0, m0, s1, m1)
        return 0

    lax.fori_loop(0, 7, pair, 0)
    act(14)
    half(15, 14, s1, m1, s0, m0)
    act(15)
    half(None, 15, None, None, s1, m1)
    act("last")

    def drain(slot, _):
        for rh in range(4):
            pltpu.make_async_remote_copy(
                src_ref=qbuf.at[rh, slot], dst_ref=qbuf.at[rh, slot], send_sem=gsend.at[rh, slot],
                recv_sem=grecv.at[rh, slot], device_id={"blk": at["x"]}, device_id_type=MESH).wait_send()
            pltpu.make_async_remote_copy(
                src_ref=sbuf.at[rh, slot], dst_ref=rbuf.at[rh, slot], send_sem=rsend.at[rh, slot],
                recv_sem=rrecv.at[rh, slot], device_id={"blk": at["x"]}, device_id_type=MESH).wait_send()
        return 0

    lax.fori_loop(1, 16, drain, 0)


def shards(n_blk, queries, cache_keys, cache_values, context_lengths, block_order):
    requests, tokens, width = queries.shape
    span, kv_local, dim = cache_keys.shape[1:]
    group_size = width // (kv_local * dim)
    rows = tokens * group_size
    n_z = n_blk // 2
    vmem = pl.BlockSpec(memory_space=pltpu.VMEM)
    smem = pl.BlockSpec(memory_space=pltpu.SMEM)
    hbm = pl.BlockSpec(memory_space=pl.ANY)
    keys = cache_keys.reshape(requests, span * kv_local, dim)
    values = cache_values.reshape(requests, span * kv_local, dim)
    pairs = requests * kv_local
    return pl.pallas_call(
        functools.partial(kernel, (n_z, span, tokens, group_size, dim)),
        out_shape=jax.ShapeDtypeStruct(queries.shape, bf16),
        in_specs=[vmem, smem, smem, hbm, hbm],
        out_specs=vmem,
        scratch_shapes=[
            pltpu.VMEM((pairs, 16, rows, dim), bf16),
            pltpu.VMEM((span * kv_local, dim), bf16),
            pltpu.VMEM((span * kv_local, dim), bf16),
            pltpu.VMEM((span * kv_local, dim), bf16),
            pltpu.VMEM((span * kv_local, dim), bf16),
            pltpu.VMEM((pairs, span, dim), bf16),
            pltpu.VMEM((pairs, dim + 16, span), bf16),
            pltpu.VMEM((span, 4 * rows), f32),
            pltpu.VMEM((span, 4 * rows), f32),
            pltpu.VMEM((1, 4 * rows), f32),
            pltpu.VMEM((1, 4 * rows), f32),
            pltpu.VMEM((requests * 4, 1, 4 * rows), jnp.int32),
            pltpu.VMEM((pairs, 16, dim, rows), f32),
            pltpu.VMEM((pairs, 16, 2, rows), f32),
            pltpu.VMEM((pairs, 16, dim + 16, rows), bf16),
            pltpu.VMEM((pairs, 16, dim + 16, rows), bf16),
            pltpu.SemaphoreType.DMA((4,)),
            pltpu.SemaphoreType.DMA((pairs, 16)),
            pltpu.SemaphoreType.DMA((pairs, 16)),
            pltpu.SemaphoreType.DMA((pairs, 16)),
            pltpu.SemaphoreType.DMA((pairs, 16)),
        ],
        compiler_params=pltpu.CompilerParams(
            collective_id=0, has_side_effects=True, vmem_limit_bytes=62 << 20
        ),
    )(queries, context_lengths, block_order, keys, values)


def solution(mesh):
    return jax.shard_map(
        functools.partial(shards, mesh.shape["blk"]),
        mesh=mesh,
        in_specs=(
            P("rep", "blk", "head"),
            P("rep", "blk", "head", None),
            P("rep", "blk", "head", None),
            P("rep"),
            P("rep", None),
        ),
        out_specs=P("rep", "blk", "head"),
        check_vma=False,
    )
```

time: 75.2 us -> 57.1 us (0.76)
  Pallas kernels: 73.1 us -> 55.4 us
    pallas_call x1, Pallas kernels: 73.1 us -> 55.4 us  [shards(): pl.pallas_call(functools.partial(kernel, (n_z, span, tokens, group_size,...]
where the time goes in v2:
time: 57.1 us; the launch traced here: 57 us
  Pallas kernels  55.4 us (97%)
  local copies, waits for them, and re-layouts  1.57 us (3%)
    pallas_call x1, Pallas kernels, shards(): pl.pallas_call(functools.partial(kernel, (n_z, span, tokens, group_size,...  55.4 us
    unnamed x1, local copies, waits for them, and re-layouts  1.57 us

profile of v2, /device:TPU:8, one launch (start us, length us, event | category | flops | bytes accessed | tf_op | source)
XLA Modules:
  0.0 57.0 jit_solution(2318866586091250384)
XLA Ops:
  0.0 55.4 %shard_map.55 = bf16[2,16,2048]{2,1,0:T(8,128)(2,1)} custom-call(bf16[2,16,2048]{2,1,0:T(8,128)(2,1)} %q_ref.1, s32[2]{0:T(128)} %lengths_ref.1, s32[2,16]{1,0:T(2,128)} %order_ref.1, bf16[2,4096,128]{2,1,0:T(8,128)(2,1)} %bitcast.2, bf16[2,4096,128]{2,1,0:T(8,128)(2,1)} %bitcast.3), custom_call_target="tpu_custom_call" | custom-call | tf_op jit(solution)/shard_map/pallas_call | solution.py:356
  55.4 1.6 %copy.7 = bf16[2,16,2048]{2,1,0:T(8,128)(2,1)} copy(bf16[2,16,2048]{2,1,0:T(8,128)(2,1)} %shard_map.55) | data formatting | bytes 262144

commit v3 on v2

--- a/solution.py
+++ b/solution.py
@@ -16,48 +16,55 @@
 slot_column = (0, 1, 0, 0, 1, 1, 0, 0, 0, 0, 1, 1, 0, 1, 1, 1)
 slot_offset = (0, 0, 1, -1, 1, -1, 2, -2, 3, -3, 2, -2, 4, 4, 3, -3)
 
-gather_trees = ("Q", "T2")
-reduce_trees = ("T2", "Q")
-groups = ((5, 12, 15, 7), (11, 8, 9, 10), (4, 13, 14, 3), (6, 0, 2, 1))
-tile_order = ((0, 3), (0, 1), (1, 3), (0, 0), (0, 2), (1, 1), (1, 0), (2, 3), (1, 2), (2, 0), (3, 3), (2, 2), (3, 0), (3, 2), (2, 1), (3, 1))
+gather_trees = (
+    (
+        ((0, "x"), (0, "up"), (0, "down"), (2, "x"), (3, "x"), (0, "up2"), (3, "down"), (6, "up"), (7, "down"), (6, "x"), (5, "down"), (8, "up"), (10, "up2"), (8, "x"), (5, "down2")),
+        ((0, "x"), (0, "up"), (0, "down"), (2, "x"), (3, "x"), (2, "up"), (0, "down2"), (6, "up"), (7, "down"), (4, "up"), (7, "x"), (9, "down"), (11, "down2"), (4, "up2"), (9, "x")),
+    ),
+    (
+        ((0, "x"), (0, "up"), (0, "down"), (1, "up"), (3, "x"), (2, "up"), (3, "down"), (6, "up"), (7, "down"), (6, "x"), (7, "x"), (6, "up2"), (12, "x"), (8, "x"), (11, "down")),
+        ((0, "x"), (0, "up"), (0, "down"), (2, "x"), (1, "down"), (2, "up"), (3, "down"), (6, "up"), (7, "down"), (6, "x"), (7, "x"), (7, "down2"), (12, "x"), (10, "up"), (9, "x")),
+    ),
+)
+reduce_trees = (
+    (
+        ((0, "x"), (0, "up"), (0, "down"), (1, "up"), (3, "x"), (2, "up"), (3, "down"), (6, "up"), (7, "down"), (6, "x"), (5, "down"), (8, "up"), (10, "up2"), (10, "up"), (5, "down2")),
+        ((0, "x"), (0, "up"), (0, "down"), (2, "x"), (1, "down"), (2, "up"), (3, "down"), (6, "up"), (7, "down"), (4, "up"), (7, "x"), (9, "down"), (11, "down2"), (4, "up2"), (11, "down")),
+    ),
+    (
+        ((0, "x"), (0, "up"), (0, "down"), (2, "x"), (3, "x"), (0, "up2"), (0, "down2"), (6, "up"), (7, "down"), (6, "x"), (7, "x"), (8, "up"), (10, "up2"), (8, "x"), (11, "down")),
+        ((0, "x"), (0, "up"), (0, "down"), (2, "x"), (3, "x"), (0, "up2"), (0, "down2"), (6, "up"), (7, "down"), (6, "x"), (7, "x"), (9, "down"), (11, "down2"), (10, "up"), (9, "x")),
+    ),
+)
+groups = ((13, 10, 8, 15), (5, 1, 7, 4), (3, 0, 2, 6), (11, 14, 12, 9))
+tile_order = ((1, 2), (0, 2), (1, 1), (1, 3), (1, 0), (3, 1), (0, 0), (0, 3), (3, 3), (2, 3), (2, 0), (3, 0), (0, 1), (3, 2), (2, 1), (2, 2))
 plan = {
-    "keys": [("f", 0, 0), ("f", 1, 0)],
+    "keys": [("f", 1, 0), ("f", 0, 0), ("f", 3, 0), ("f", 2, 0)],
     "values": [],
-    "first": [("f", 0, 1), ("f", 0, 6), ("f", 0, 7), ("f", 1, 1), ("w", 0, 2)],
-    0: [("f", 2, 0), ("f", 3, 0), ("f", 1, 6), ("f", 1, 7), ("f", 0, 8), ("f", 0, 9), ("w", 0, 11), ("w", 0, 10)],
-    1: [("f", 0, 12), ("f", 2, 1), ("f", 2, 3), ("f", 3, 1), ("f", 3, 3), ("w", 1, 2)],
-    2: [("f", 1, 9), ("f", 2, 2), ("r", 0, 11), ("r", 0, 10), ("f", 3, 2), ("w", 0, 5), ("w", 0, 15)],
-    3: [("f", 1, 8), ("f", 1, 12), ("w", 0, 4), ("w", 0, 13), ("w", 0, 14), ("w", 0, 3)],
-    4: [("f", 2, 4), ("f", 2, 7), ("r", 0, 15), ("r", 0, 5), ("w", 1, 11), ("w", 1, 10)],
-    5: [("f", 2, 6), ("r", 0, 14), ("r", 0, 13), ("f", 3, 5), ("f", 3, 6), ("f", 3, 7), ("r", 0, 4), ("w", 1, 5), ("w", 1, 15)],
-    6: [("f", 2, 9), ("r", 1, 11), ("r", 1, 10)],
-    7: [("f", 2, 8), ("r", 0, 9), ("r", 0, 8), ("r", 1, 15), ("w", 1, 4), ("w", 1, 13), ("w", 1, 14), ("w", 1, 3)],
-    8: [("f", 2, 12), ("r", 0, 12), ("f", 3, 9), ("f", 3, 8), ("r", 2, 2), ("f", 3, 12), ("w", 2, 5), ("w", 2, 15)],
-    9: [("r", 0, 1), ("r", 1, 14), ("r", 1, 13), ("r", 1, 5), ("r", 1, 4), ("r", 0, 7)],
-    10: [("r", 1, 9), ("r", 2, 15), ("r", 2, 5), ("w", 2, 13), ("w", 2, 14)],
-    11: [("r", 0, 6), ("r", 3, 2), ("w", 3, 15)],
-    12: [("r", 0, 3), ("r", 1, 1), ("r", 2, 14), ("r", 2, 13), ("r", 2, 4), ("r", 2, 3), ("w", 3, 4), ("w", 3, 13), ("w", 3, 14)],
-    13: [("r", 1, 8), ("r", 3, 15), ("r", 3, 5), ("w", 2, 11), ("w", 2, 10)],
-    14: [("r", 0, 2), ("r", 1, 12), ("r", 3, 14), ("r", 3, 13), ("r", 3, 4), ("r", 3, 3), ("w", 3, 11), ("w", 3, 10)],
-    15: [("r", 2, 11), ("r", 2, 10), ("r", 2, 9), ("r", 2, 8), ("r", 2, 1)],
-    "last": [("r", 1, 6), ("r", 2, 12), ("r", 3, 11), ("r", 3, 10), ("r", 3, 9), ("r", 0, 0), ("r", 3, 8), ("r", 3, 1), ("r", 1, 7), ("r", 3, 12), ("r", 1, 2), ("r", 2, 7), ("r", 2, 6), ("r", 1, 3), ("r", 3, 6), ("r", 3, 7), ("r", 2, 0), ("r", 1, 0), ("r", 3, 0)],
+    "first": [("f", 1, 2), ("f", 1, 7), ("f", 0, 6), ("f", 1, 3), ("f", 3, 1), ("f", 0, 2), ("f", 0, 3), ("f", 2, 1), ("f", 3, 2), ("f", 3, 3), ("f", 1, 4), ("f", 2, 2), ("f", 2, 3), ("f", 1, 11), ("f", 1, 6), ("f", 1, 9)],
+    0: [("f", 0, 8), ("f", 0, 10)],
+    1: [("f", 0, 5), ("f", 0, 7), ("f", 3, 6), ("f", 3, 7), ("f", 2, 7), ("w", 1, 5), ("w", 1, 1)],
+    2: [("f", 2, 6), ("w", 1, 14), ("w", 1, 12)],
+    3: [("f", 3, 10), ("r", 1, 5), ("w", 1, 13), ("w", 1, 10), ("w", 1, 8), ("w", 1, 15)],
+    4: [("r", 1, 12), ("r", 1, 14), ("f", 2, 11), ("w", 3, 5), ("w", 3, 4)],
+    5: [("f", 3, 9), ("r", 1, 15), ("r", 1, 13), ("r", 1, 10), ("r", 1, 8), ("f", 2, 8), ("w", 0, 13), ("w", 0, 15)],
+    6: [("f", 3, 12), ("f", 2, 12), ("r", 3, 5), ("r", 3, 4), ("r", 3, 1), ("w", 0, 11), ("w", 0, 14), ("w", 0, 12), ("w", 0, 9)],
+    7: [("r", 1, 1), ("r", 0, 13), ("r", 0, 15), ("w", 3, 11), ("w", 3, 14)],
+    8: [("r", 1, 9), ("r", 0, 14), ("r", 0, 12), ("r", 0, 11), ("r", 0, 9), ("w", 2, 14), ("w", 2, 9)],
+    9: [("r", 1, 6), ("r", 1, 4), ("r", 3, 14), ("r", 3, 12), ("w", 2, 13), ("w", 2, 10), ("w", 2, 15)],
+    10: [("r", 1, 11), ("r", 2, 14), ("r", 2, 12), ("r", 2, 9), ("w", 3, 13), ("w", 3, 8), ("w", 3, 15)],
+    11: [("r", 0, 10), ("r", 2, 15), ("r", 2, 13), ("r", 0, 8), ("w", 0, 1), ("w", 0, 4)],
+    12: [("r", 1, 2), ("r", 3, 15), ("r", 3, 13), ("r", 3, 8)],
+    13: [("r", 1, 7), ("r", 0, 7), ("r", 0, 5), ("r", 0, 4), ("r", 3, 10), ("r", 2, 8), ("w", 2, 5), ("w", 2, 4)],
+    14: [("r", 3, 3), ("r", 3, 2), ("r", 2, 11), ("r", 2, 10)],
+    15: [("r", 0, 6), ("r", 3, 11), ("r", 3, 9), ("r", 2, 5), ("r", 2, 4), ("r", 2, 1)],
+    "last": [("r", 1, 3), ("r", 3, 6), ("r", 0, 3), ("r", 0, 1), ("r", 2, 7), ("r", 2, 6), ("r", 3, 7), ("r", 0, 2), ("r", 1, 0), ("r", 2, 3), ("r", 2, 2), ("r", 0, 0), ("r", 3, 0), ("r", 2, 0)],
 }
-split_steps = (1, 6)
+split_steps = (1, 2)
 
 
 def edge(tree, slot, head):
-    table = {
-        1: (0, "x"), 2: (0, "up"), 3: (0, "down"), 4: (1, "up"), 5: (1, "down"), 6: (2, "up"), 7: (3, "down"),
-        8: (6, "up"), 9: (7, "down"), 10: (6, "x"), 11: (7, "x"), 13: (12, "x"), 14: (8, "x"), 15: (9, "x"),
-        12: (6, "up2") if head == 0 else (7, "down2"),
-    }
-    if tree == "Q":
-        table.update({6: (0, "up2"), 7: (0, "down2")})
-    if tree in ("M", "M2"):
-        table[12] = (8, "up") if head == 0 else (9, "down")
-    if tree in ("M2", "T2"):
-        table.update({10: (4, "up")} if head == 0 else {11: (5, "down")})
-    return table[slot]
+    return tree[head][slot - 1]
 
 
 opposite = {"x": "x", "up": "down", "down": "up", "up2": "down2", "down2": "up2"}
@@ -80,9 +87,9 @@
 group_code = signed(packed([g for rh, g in tile_order]))
 
 
-def kernel(sizes, q_ref, lengths_ref, order_ref, k_hbm, v_hbm, out_ref,
-           qbuf, kraw0, kraw1, vraw0, vraw1, kp, vt, s0, s1, m0, m1, qrel, part, stats, sbuf, rbuf,
-           load_sem, gsend, grecv, rsend, rrecv):
+def kernel(sizes, q_hbm, lengths_ref, order_ref, k_hbm, v_hbm, out_hbm,
+           q_ref, out_ref, qbuf, kraw0, kraw1, vraw0, vraw1, kp, vt, s0, s1, m0, m1, qrel, part, stats, sbuf, rbuf,
+           load_sem, out_sem, gsend, grecv, rsend, rrecv):
     n_z, span, tokens, group_size, dim = sizes
     rows = tokens * group_size
     chunk = 256
@@ -100,6 +107,8 @@
     }
     kraw, vraw = (kraw0, kraw1), (vraw0, vraw1)
 
+    q_load = pltpu.make_async_copy(q_hbm, q_ref, load_sem.at[4])
+    q_load.start()
     loads = []
     for r in range(2):
         for i, (src, dst) in enumerate(((k_hbm, kraw), (v_hbm, vraw))):
@@ -110,6 +119,7 @@
     for name in at:
         pl.semaphore_signal(barrier, inc=1, device_id={"blk": at[name]}, device_id_type=MESH)
 
+    q_load.wait()
     for r in range(2):
         for h in range(2):
             for g in range(group_size):
@@ -282,13 +292,30 @@
         for g in range(group_size):
             begin = (rh % 2 * group_size + g) * dim
             out_ref[rh // 2, :, pl.ds(begin, dim)] = result[g * tokens : (g + 1) * tokens]
+        store(rh).start()
+
+    def store(rh):
+        where = pl.ds(rh % 2 * group_size * dim, group_size * dim)
+        return pltpu.make_async_copy(out_ref.at[rh // 2, :, where], out_hbm.at[rh // 2, :, where], out_sem.at[rh])
+
+    def drain(slot, _):
+        for rh in range(4):
+            pltpu.make_async_remote_copy(
+                src_ref=qbuf.at[rh, slot], dst_ref=qbuf.at[rh, slot], send_sem=gsend.at[rh, slot],
+                recv_sem=grecv.at[rh, slot], device_id={"blk": at["x"]}, device_id_type=MESH).wait_send()
+            pltpu.make_async_remote_copy(
+                src_ref=sbuf.at[rh, slot], dst_ref=rbuf.at[rh, slot], send_sem=rsend.at[rh, slot],
+                recv_sem=rrecv.at[rh, slot], device_id={"blk": at["x"]}, device_id_type=MESH).wait_send()
+        return 0
 
     def act(step):
         if step in split_steps:
             i = split_steps.index(step)
             loads[2 + i].wait()
             (split_keys, split_values)[i](1)
-        for kind, rh, slot in plan[step]:
+        for i, (kind, rh, slot) in enumerate(plan[step]):
+            if step == "last" and plan[step][i:] == [("r", rh, 0)]:
+                lax.fori_loop(1, 16, drain, 0)
             if kind == "w":
                 gather_copy(rh, slot).wait_recv()
             elif kind == "f":
@@ -328,17 +355,8 @@
     half(None, 15, None, None, s1, m1)
     act("last")
 
-    def drain(slot, _):
-        for rh in range(4):
-            pltpu.make_async_remote_copy(
-                src_ref=qbuf.at[rh, slot], dst_ref=qbuf.at[rh, slot], send_sem=gsend.at[rh, slot],
-                recv_sem=grecv.at[rh, slot], device_id={"blk": at["x"]}, device_id_type=MESH).wait_send()
-            pltpu.make_async_remote_copy(
-                src_ref=sbuf.at[rh, slot], dst_ref=rbuf.at[rh, slot], send_sem=rsend.at[rh, slot],
-                recv_sem=rrecv.at[rh, slot], device_id={"blk": at["x"]}, device_id_type=MESH).wait_send()
-        return 0
-
-    lax.fori_loop(1, 16, drain, 0)
+    for rh in range(4):
+        store(rh).wait()
 
 
 def shards(n_blk, queries, cache_keys, cache_values, context_lengths, block_order):
@@ -347,7 +365,6 @@
     group_size = width // (kv_local * dim)
     rows = tokens * group_size
     n_z = n_blk // 2
-    vmem = pl.BlockSpec(memory_space=pltpu.VMEM)
     smem = pl.BlockSpec(memory_space=pltpu.SMEM)
     hbm = pl.BlockSpec(memory_space=pl.ANY)
     keys = cache_keys.reshape(requests, span * kv_local, dim)
@@ -356,9 +373,11 @@
     return pl.pallas_call(
         functools.partial(kernel, (n_z, span, tokens, group_size, dim)),
         out_shape=jax.ShapeDtypeStruct(queries.shape, bf16),
-        in_specs=[vmem, smem, smem, hbm, hbm],
-        out_specs=vmem,
+        in_specs=[hbm, smem, smem, hbm, hbm],
+        out_specs=hbm,
         scratch_shapes=[
+            pltpu.VMEM(queries.shape, bf16),
+            pltpu.VMEM(queries.shape, bf16),
             pltpu.VMEM((pairs, 16, rows, dim), bf16),
             pltpu.VMEM((span * kv_local, dim), bf16),
             pltpu.VMEM((span * kv_local, dim), bf16),
@@ -375,7 +394,8 @@
             pltpu.VMEM((pairs, 16, 2, rows), f32),
             pltpu.VMEM((pairs, 16, dim + 16, rows), bf16),
             pltpu.VMEM((pairs, 16, dim + 16, rows), bf16),
-            pltpu.SemaphoreType.DMA((4,)),
+            pltpu.SemaphoreType.DMA((5,)),
+            pltpu.SemaphoreType.DMA((pairs,)),
             pltpu.SemaphoreType.DMA((pairs, 16)),
             pltpu.SemaphoreType.DMA((pairs, 16)),
             pltpu.SemaphoreType.DMA((pairs, 16)),

time: 57.1 us -> 52.7 us (0.923)
  Pallas kernels: 55.4 us -> 51 us
    pallas_call x1, Pallas kernels: 55.4 us -> 51 us  [shards(): pl.pallas_call(functools.partial(kernel, (n_z, span, tokens, group_size,...]
where the time goes in v3:
time: 52.7 us; the launch traced here: 52.6 us
  Pallas kernels  51 us (97%)
  local copies, waits for them, and re-layouts  1.57 us (3%)
    pallas_call x1, Pallas kernels, shards(): pl.pallas_call(functools.partial(kernel, (n_z, span, tokens, group_size,...  51 us
    unnamed x1, local copies, waits for them, and re-layouts  1.57 us

profile of v3, /device:TPU:8, one launch (start us, length us, event | category | flops | bytes accessed | tf_op | source)
XLA Modules:
  0.0 52.6 jit_solution(1260235640599113772)
XLA Ops:
  0.0 51.0 %shard_map.55 = bf16[2,16,2048]{2,1,0:T(8,128)(2,1)} custom-call(bf16[2,16,2048]{2,1,0:T(8,128)(2,1)} %q_hbm.1, s32[2]{0:T(128)} %lengths_ref.1, s32[2,16]{1,0:T(2,128)} %order_ref.1, bf16[2,4096,128]{2,1,0:T(8,128)(2,1)} %bitcast.2, bf16[2,4096,128]{2,1,0:T(8,128)(2,1)} %bitcast.3), custom_call_target="tpu_custom_call" | custom-call | tf_op jit(solution)/shard_map/pallas_call | solution.py:373
  51.0 1.6 %copy.7 = bf16[2,16,2048]{2,1,0:T(8,128)(2,1)} copy(bf16[2,16,2048]{2,1,0:T(8,128)(2,1)} %shard_map.55) | data formatting | bytes 262144

commit v4 on v3

--- a/solution.py
+++ b/solution.py
@@ -17,62 +17,65 @@
 slot_offset = (0, 0, 1, -1, 1, -1, 2, -2, 3, -3, 2, -2, 4, 4, 3, -3)
 
 gather_trees = (
-    (
-        ((0, "x"), (0, "up"), (0, "down"), (2, "x"), (3, "x"), (0, "up2"), (3, "down"), (6, "up"), (7, "down"), (6, "x"), (5, "down"), (8, "up"), (10, "up2"), (8, "x"), (5, "down2")),
-        ((0, "x"), (0, "up"), (0, "down"), (2, "x"), (3, "x"), (2, "up"), (0, "down2"), (6, "up"), (7, "down"), (4, "up"), (7, "x"), (9, "down"), (11, "down2"), (4, "up2"), (9, "x")),
-    ),
-    (
-        ((0, "x"), (0, "up"), (0, "down"), (1, "up"), (3, "x"), (2, "up"), (3, "down"), (6, "up"), (7, "down"), (6, "x"), (7, "x"), (6, "up2"), (12, "x"), (8, "x"), (11, "down")),
-        ((0, "x"), (0, "up"), (0, "down"), (2, "x"), (1, "down"), (2, "up"), (3, "down"), (6, "up"), (7, "down"), (6, "x"), (7, "x"), (7, "down2"), (12, "x"), (10, "up"), (9, "x")),
-    ),
+    ((0, "x"), (0, "up"), (0, "down"), (1, "up"), (3, "x"), (0, "up2"), (3, "down"), (6, "up"), (7, "down"), (6, "x"), (5, "down"), (6, "up2"), (12, "x"), (10, "up"), (9, "x")),
+    ((0, "x"), (0, "up"), (0, "down"), (2, "x"), (3, "x"), (2, "up"), (3, "down"), (6, "up"), (7, "down"), (4, "up"), (7, "x"), (9, "down"), (11, "down2"), (4, "up2"), (11, "down")),
+    ((0, "x"), (0, "up"), (0, "down"), (2, "x"), (3, "x"), (2, "up"), (3, "down"), (6, "up"), (7, "down"), (6, "x"), (5, "down"), (7, "down2"), (12, "x"), (4, "up2"), (9, "x")),
+    ((0, "x"), (0, "up"), (0, "down"), (2, "x"), (3, "x"), (2, "up"), (3, "down"), (6, "up"), (3, "down2"), (6, "x"), (7, "x"), (9, "down"), (12, "x"), (8, "x"), (9, "x")),
 )
 reduce_trees = (
-    (
-        ((0, "x"), (0, "up"), (0, "down"), (1, "up"), (3, "x"), (2, "up"), (3, "down"), (6, "up"), (7, "down"), (6, "x"), (5, "down"), (8, "up"), (10, "up2"), (10, "up"), (5, "down2")),
-        ((0, "x"), (0, "up"), (0, "down"), (2, "x"), (1, "down"), (2, "up"), (3, "down"), (6, "up"), (7, "down"), (4, "up"), (7, "x"), (9, "down"), (11, "down2"), (4, "up2"), (11, "down")),
-    ),
-    (
-        ((0, "x"), (0, "up"), (0, "down"), (2, "x"), (3, "x"), (0, "up2"), (0, "down2"), (6, "up"), (7, "down"), (6, "x"), (7, "x"), (8, "up"), (10, "up2"), (8, "x"), (11, "down")),
-        ((0, "x"), (0, "up"), (0, "down"), (2, "x"), (3, "x"), (0, "up2"), (0, "down2"), (6, "up"), (7, "down"), (6, "x"), (7, "x"), (9, "down"), (11, "down2"), (10, "up"), (9, "x")),
-    ),
+    ((0, "x"), (0, "up"), (0, "down"), (2, "x"), (3, "x"), (2, "up"), (3, "down"), (6, "up"), (7, "down"), (6, "x"), (5, "down"), (8, "up"), (10, "up2"), (8, "x"), (11, "down")),
+    ((0, "x"), (0, "up"), (0, "down"), (2, "x"), (1, "down"), (2, "up"), (0, "down2"), (6, "up"), (7, "down"), (6, "x"), (7, "x"), (9, "down"), (15, "down"), (10, "up"), (9, "x")),
+    ((0, "x"), (0, "up"), (0, "down"), (2, "x"), (3, "x"), (2, "up"), (3, "down"), (6, "up"), (7, "down"), (4, "up"), (7, "x"), (7, "down2"), (12, "x"), (10, "up"), (11, "down")),
+    ((0, "x"), (0, "up"), (0, "down"), (1, "up"), (1, "down"), (0, "up2"), (0, "down2"), (6, "up"), (7, "down"), (6, "x"), (5, "down"), (6, "up2"), (14, "up"), (8, "x"), (11, "down")),
 )
-groups = ((13, 10, 8, 15), (5, 1, 7, 4), (3, 0, 2, 6), (11, 14, 12, 9))
-tile_order = ((1, 2), (0, 2), (1, 1), (1, 3), (1, 0), (3, 1), (0, 0), (0, 3), (3, 3), (2, 3), (2, 0), (3, 0), (0, 1), (3, 2), (2, 1), (2, 2))
+groups = (
+    ((14, 15, 9, 13), (8, 11, 2, 4), (10, 7, 12, 6), (1, 5, 3, 0)),
+    ((13, 14, 9, 7), (3, 1, 0, 2), (5, 11, 6, 4), (8, 12, 15, 10)),
+    ((12, 8, 10, 11), (9, 14, 13, 15), (0, 6, 5, 4), (1, 3, 2, 7)),
+    ((13, 10, 8, 5), (3, 15, 1, 7), (6, 14, 11, 12), (4, 2, 0, 9)),
+)
+tile_order = ((1, 1), (0, 3), (0, 2), (3, 3), (0, 1), (3, 1), (0, 0), (3, 0), (1, 0), (2, 1), (3, 2), (1, 3), (2, 0), (2, 2), (1, 2), (2, 3))
+send_rank = (
+    (3, 2, 3, 1, 3, 5, 1, 2, 4, 0, 0, 4, 0, 4, 4, 5),
+    (5, 3, 3, 2, 0, 2, 1, 1, 4, 5, 5, 5, 1, 4, 0, 1),
+    (2, 0, 5, 0, 3, 1, 2, 3, 5, 2, 1, 4, 2, 2, 0, 2),
+    (0, 4, 5, 1, 3, 3, 1, 4, 2, 1, 5, 1, 3, 2, 5, 5),
+)
 plan = {
-    "keys": [("f", 1, 0), ("f", 0, 0), ("f", 3, 0), ("f", 2, 0)],
+    "keys": [("f", 0, 0), ("f", 1, 0), ("f", 3, 0), ("f", 2, 0)],
     "values": [],
-    "first": [("f", 1, 2), ("f", 1, 7), ("f", 0, 6), ("f", 1, 3), ("f", 3, 1), ("f", 0, 2), ("f", 0, 3), ("f", 2, 1), ("f", 3, 2), ("f", 3, 3), ("f", 1, 4), ("f", 2, 2), ("f", 2, 3), ("f", 1, 11), ("f", 1, 6), ("f", 1, 9)],
-    0: [("f", 0, 8), ("f", 0, 10)],
-    1: [("f", 0, 5), ("f", 0, 7), ("f", 3, 6), ("f", 3, 7), ("f", 2, 7), ("w", 1, 5), ("w", 1, 1)],
-    2: [("f", 2, 6), ("w", 1, 14), ("w", 1, 12)],
-    3: [("f", 3, 10), ("r", 1, 5), ("w", 1, 13), ("w", 1, 10), ("w", 1, 8), ("w", 1, 15)],
-    4: [("r", 1, 12), ("r", 1, 14), ("f", 2, 11), ("w", 3, 5), ("w", 3, 4)],
-    5: [("f", 3, 9), ("r", 1, 15), ("r", 1, 13), ("r", 1, 10), ("r", 1, 8), ("f", 2, 8), ("w", 0, 13), ("w", 0, 15)],
-    6: [("f", 3, 12), ("f", 2, 12), ("r", 3, 5), ("r", 3, 4), ("r", 3, 1), ("w", 0, 11), ("w", 0, 14), ("w", 0, 12), ("w", 0, 9)],
-    7: [("r", 1, 1), ("r", 0, 13), ("r", 0, 15), ("w", 3, 11), ("w", 3, 14)],
-    8: [("r", 1, 9), ("r", 0, 14), ("r", 0, 12), ("r", 0, 11), ("r", 0, 9), ("w", 2, 14), ("w", 2, 9)],
-    9: [("r", 1, 6), ("r", 1, 4), ("r", 3, 14), ("r", 3, 12), ("w", 2, 13), ("w", 2, 10), ("w", 2, 15)],
-    10: [("r", 1, 11), ("r", 2, 14), ("r", 2, 12), ("r", 2, 9), ("w", 3, 13), ("w", 3, 8), ("w", 3, 15)],
-    11: [("r", 0, 10), ("r", 2, 15), ("r", 2, 13), ("r", 0, 8), ("w", 0, 1), ("w", 0, 4)],
-    12: [("r", 1, 2), ("r", 3, 15), ("r", 3, 13), ("r", 3, 8)],
-    13: [("r", 1, 7), ("r", 0, 7), ("r", 0, 5), ("r", 0, 4), ("r", 3, 10), ("r", 2, 8), ("w", 2, 5), ("w", 2, 4)],
-    14: [("r", 3, 3), ("r", 3, 2), ("r", 2, 11), ("r", 2, 10)],
-    15: [("r", 0, 6), ("r", 3, 11), ("r", 3, 9), ("r", 2, 5), ("r", 2, 4), ("r", 2, 1)],
-    "last": [("r", 1, 3), ("r", 3, 6), ("r", 0, 3), ("r", 0, 1), ("r", 2, 7), ("r", 2, 6), ("r", 3, 7), ("r", 0, 2), ("r", 1, 0), ("r", 2, 3), ("r", 2, 2), ("r", 0, 0), ("r", 3, 0), ("r", 2, 0)],
+    "first": [("f", 0, 3), ("f", 0, 1), ("f", 1, 3), ("f", 0, 6), ("f", 3, 3), ("f", 2, 3), ("f", 1, 2), ("w", 1, 1)],
+    0: [("f", 3, 2), ("f", 0, 7), ("f", 0, 5)],
+    1: [("r", 1, 3), ("f", 2, 2), ("f", 1, 7), ("f", 0, 10), ("f", 3, 9), ("f", 0, 12)],
+    2: [("f", 1, 4), ("f", 3, 7), ("f", 2, 7), ("r", 0, 1), ("f", 1, 6), ("f", 2, 5), ("f", 0, 9), ("w", 3, 4)],
+    3: [("f", 1, 11), ("f", 3, 6), ("f", 3, 12), ("f", 1, 9), ("f", 2, 4), ("r", 0, 12), ("f", 2, 6), ("w", 0, 8), ("w", 0, 11), ("w", 0, 2), ("w", 0, 4)],
+    4: [("r", 3, 4), ("f", 2, 9), ("r", 3, 9), ("r", 3, 2), ("w", 3, 15), ("w", 3, 1)],
+    5: [("f", 2, 12), ("r", 0, 4), ("w", 0, 14), ("w", 0, 15), ("w", 0, 13)],
+    6: [("r", 3, 15), ("r", 3, 3), ("f", 3, 8), ("w", 3, 13), ("w", 3, 10), ("w", 3, 5)],
+    7: [("r", 0, 14), ("r", 0, 15), ("r", 0, 13), ("r", 0, 9), ("w", 1, 13), ("w", 1, 14)],
+    8: [("r", 3, 13), ("r", 3, 10), ("r", 3, 7), ("w", 2, 14), ("w", 2, 13), ("w", 2, 15)],
+    9: [("r", 1, 13), ("r", 1, 14), ("w", 3, 14), ("w", 3, 11)],
+    10: [("r", 0, 8), ("r", 0, 10), ("r", 2, 9), ("r", 2, 14), ("r", 2, 15), ("r", 0, 11), ("r", 2, 13), ("r", 0, 7), ("w", 1, 8), ("w", 1, 12), ("w", 1, 15), ("w", 1, 10)],
+    11: [("r", 3, 14), ("r", 3, 11), ("r", 3, 12), ("w", 2, 8), ("w", 2, 10), ("w", 2, 11)],
+    12: [("r", 1, 8), ("r", 1, 10), ("r", 1, 15), ("r", 1, 12)],
+    13: [("r", 2, 10), ("r", 2, 11), ("r", 0, 6), ("r", 2, 8), ("r", 2, 12), ("w", 1, 5)],
+    14: [("r", 0, 5), ("r", 2, 5), ("r", 3, 8), ("w", 2, 1)],
+    15: [("r", 1, 9), ("r", 3, 5), ("r", 1, 6), ("r", 1, 11), ("r", 1, 4), ("r", 1, 5)],
+    "last": [("r", 2, 4), ("r", 2, 1), ("r", 0, 2), ("r", 2, 7), ("r", 0, 3), ("r", 2, 6), ("r", 3, 6), ("r", 1, 7), ("r", 3, 1), ("r", 1, 2), ("r", 1, 1), ("r", 2, 2), ("r", 2, 3), ("r", 0, 0), ("r", 3, 0), ("r", 1, 0), ("r", 2, 0)],
 }
-split_steps = (1, 2)
-
-
-def edge(tree, slot, head):
-    return tree[head][slot - 1]
+split_steps = ("first", 3)
+
+
+def edge(tree, slot):
+    return tree[slot - 1]
 
 
 opposite = {"x": "x", "up": "down", "down": "up", "up2": "down2", "down2": "up2"}
-place = {slot: 4 * g + i for g, slots in enumerate(groups) for i, slot in enumerate(slots)}
-
-
-def children(tree, slot, head):
-    return [b for b in range(1, 16) if edge(tree, b, head)[0] == slot]
+place = [{slot: 4 * g + i for g, slots in enumerate(own) for i, slot in enumerate(slots)} for own in groups]
+
+
+def children(tree, slot):
+    return [b for b in range(1, 16) if edge(tree, b)[0] == slot]
 
 
 def packed(values):
@@ -124,28 +127,27 @@
         for h in range(2):
             for g in range(group_size):
                 begin = (h * group_size + g) * dim
-                qbuf[2 * r + h, place[0], pl.ds(g * tokens, tokens), :] = q_ref[r, :, pl.ds(begin, dim)]
+                qbuf[2 * r + h, place[2 * r + h][0], pl.ds(g * tokens, tokens), :] = q_ref[r, :, pl.ds(begin, dim)]
     pl.semaphore_wait(barrier, len(at))
 
     def gather_copy(rh, slot):
-        parent, name = edge(gather_trees[rh // 2], slot, rh % 2)
+        parent, name = edge(gather_trees[rh], slot)
         return pltpu.make_async_remote_copy(
-            src_ref=qbuf.at[rh, place[parent]], dst_ref=qbuf.at[rh, place[slot]],
+            src_ref=qbuf.at[rh, place[rh][parent]], dst_ref=qbuf.at[rh, place[rh][slot]],
             send_sem=gsend.at[rh, slot], recv_sem=grecv.at[rh, slot],
             device_id={"blk": at[opposite[name]]}, device_id_type=MESH)
 
     def reduce_copy(rh, slot):
-        parent, name = edge(reduce_trees[rh // 2], slot, rh % 2)
+        parent, name = edge(reduce_trees[rh], slot)
         return pltpu.make_async_remote_copy(
-            src_ref=sbuf.at[rh, place[slot]], dst_ref=rbuf.at[rh, slot],
+            src_ref=sbuf.at[rh, place[rh][slot]], dst_ref=rbuf.at[rh, slot],
             send_sem=rsend.at[rh, slot], recv_sem=rrecv.at[rh, slot],
             device_id={"blk": at[name]}, device_id_type=MESH)
 
     def forward(rh, slot):
-        tree = gather_trees[rh // 2]
         if slot:
             gather_copy(rh, slot).wait_recv()
-        for child in sorted(children(tree, slot, rh % 2), key=lambda b: -len(children(tree, b, rh % 2))):
+        for child in sorted(children(gather_trees[rh], slot), key=lambda b: (send_rank[rh][b], b)):
             gather_copy(rh, child).start()
 
     first, limits = [], []
@@ -160,7 +162,9 @@
                 owner_column = column if slot_column[slot] == 0 else 1 - column
                 owner = owner_column * n_z + lax.rem(z + slot_offset[slot] + n_z, n_z)
                 begin = base + order_ref[r, owner] * tokens - first[r] * chunk
-                qrel[4 * r + place[slot] // 4, :, pl.ds(place[slot] % 4 * rows, rows)] = lane_token + begin
+                for h in range(2):
+                    spot = place[2 * r + h][slot]
+                    qrel[4 * (2 * r + h) + spot // 4, :, pl.ds(spot % 4 * rows, rows)] = lane_token + begin
 
     row_index = lax.broadcasted_iota(jnp.int32, (256, 256), 0)
     col_index = lax.broadcasted_iota(jnp.int32, (256, 256), 1)
@@ -226,7 +230,7 @@
         if following is not None:
             key_at, g = tile(following)
             q = qbuf[key_at, pl.ds(g * 4, 4)].reshape(4 * rows, dim)
-            limit = qrel[4 * (key_at >> 1) + g]
+            limit = qrel[4 * key_at + g]
             top = None
         if current is not None:
             now_at, gc = tile(current)
@@ -266,8 +270,8 @@
         sbuf[rh, spot, pl.ds(dim, 16), :] = tail.astype(bf16)
 
     def merged(rh, slot, kids):
-        own = stats[rh, place[slot]]
-        tops, totals, sums = [own[0:1]], [own[1:2]], [part[rh, place[slot]]]
+        own = stats[rh, place[rh][slot]]
+        tops, totals, sums = [own[0:1]], [own[1:2]], [part[rh, place[rh][slot]]]
         for child in kids:
             reduce_copy(rh, child).wait_recv()
             tail = rbuf[rh, child, pl.ds(dim, 16), :].astype(f32)
@@ -281,10 +285,10 @@
         return o, top, total
 
     def send_back(rh, slot):
-        kids = children(reduce_trees[rh // 2], slot, rh % 2)
+        kids = children(reduce_trees[rh], slot)
         if slot:
             if kids:
-                put(rh, place[slot], *merged(rh, slot, kids))
+                put(rh, place[rh][slot], *merged(rh, slot, kids))
             reduce_copy(rh, slot).start()
             return
         o, top, total = merged(rh, slot, kids)
@@ -309,10 +313,10 @@
         return 0
 
     def act(step):
-        if step in split_steps:
-            i = split_steps.index(step)
-            loads[2 + i].wait()
-            (split_keys, split_values)[i](1)
+        for i, when in enumerate(split_steps):
+            if step == when:
+                loads[2 + i].wait()
+                (split_keys, split_values)[i](1)
         for i, (kind, rh, slot) in enumerate(plan[step]):
             if step == "last" and plan[step][i:] == [("r", rh, 0)]:
                 lax.fori_loop(1, 16, drain, 0)
@@ -389,7 +393,7 @@
             pltpu.VMEM((span, 4 * rows), f32),
             pltpu.VMEM((1, 4 * rows), f32),
             pltpu.VMEM((1, 4 * rows), f32),
-            pltpu.VMEM((requests * 4, 1, 4 * rows), jnp.int32),
+            pltpu.VMEM((pairs * 4, 1, 4 * rows), jnp.int32),
             pltpu.VMEM((pairs, 16, dim, rows), f32),
             pltpu.VMEM((pairs, 16, 2, rows), f32),
             pltpu.VMEM((pairs, 16, dim + 16, rows), bf16),

time: 52.7 us -> 51.3 us (0.973)
  Pallas kernels: 51 us -> 49.4 us
    pallas_call x1, Pallas kernels: 51 us -> 49.4 us  [shards(): pl.pallas_call(functools.partial(kernel, (n_z, span, tokens, group_size,...]
where the time goes in v4:
time: 51.3 us; the launch traced here: 50.9 us
  Pallas kernels  49.4 us (96%)
  local copies, waits for them, and re-layouts  1.57 us (3%)
    pallas_call x1, Pallas kernels, shards(): pl.pallas_call(functools.partial(kernel, (n_z, span, tokens, group_size,...  49.4 us
    unnamed x1, local copies, waits for them, and re-layouts  1.57 us

profile of v4, /device:TPU:8, one launch (start us, length us, event | category | flops | bytes accessed | tf_op | source)
XLA Modules:
  0.0 50.9 jit_solution(7549784263242648962)
XLA Ops:
  0.0 49.4 %shard_map.55 = bf16[2,16,2048]{2,1,0:T(8,128)(2,1)} custom-call(bf16[2,16,2048]{2,1,0:T(8,128)(2,1)} %q_hbm.1, s32[2]{0:T(128)} %lengths_ref.1, s32[2,16]{1,0:T(2,128)} %order_ref.1, bf16[2,4096,128]{2,1,0:T(8,128)(2,1)} %bitcast.2, bf16[2,4096,128]{2,1,0:T(8,128)(2,1)} %bitcast.3), custom_call_target="tpu_custom_call" | custom-call | tf_op jit(solution)/shard_map/pallas_call | solution.py:377
  49.4 1.6 %copy.7 = bf16[2,16,2048]{2,1,0:T(8,128)(2,1)} copy(bf16[2,16,2048]{2,1,0:T(8,128)(2,1)} %shard_map.55) | data formatting | bytes 262144

commit v5 on v4

--- a/solution.py
+++ b/solution.py
@@ -17,53 +17,53 @@
 slot_offset = (0, 0, 1, -1, 1, -1, 2, -2, 3, -3, 2, -2, 4, 4, 3, -3)
 
 gather_trees = (
-    ((0, "x"), (0, "up"), (0, "down"), (1, "up"), (3, "x"), (0, "up2"), (3, "down"), (6, "up"), (7, "down"), (6, "x"), (5, "down"), (6, "up2"), (12, "x"), (10, "up"), (9, "x")),
-    ((0, "x"), (0, "up"), (0, "down"), (2, "x"), (3, "x"), (2, "up"), (3, "down"), (6, "up"), (7, "down"), (4, "up"), (7, "x"), (9, "down"), (11, "down2"), (4, "up2"), (11, "down")),
-    ((0, "x"), (0, "up"), (0, "down"), (2, "x"), (3, "x"), (2, "up"), (3, "down"), (6, "up"), (7, "down"), (6, "x"), (5, "down"), (7, "down2"), (12, "x"), (4, "up2"), (9, "x")),
-    ((0, "x"), (0, "up"), (0, "down"), (2, "x"), (3, "x"), (2, "up"), (3, "down"), (6, "up"), (3, "down2"), (6, "x"), (7, "x"), (9, "down"), (12, "x"), (8, "x"), (9, "x")),
+    ((0, "x"), (0, "up"), (0, "down"), (1, "up"), (3, "x"), (0, "up2"), (3, "down"), (6, "up"), (3, "down2"), (6, "x"), (7, "x"), (8, "up"), (12, "x"), (8, "x"), (9, "x")),
+    ((0, "x"), (0, "up"), (0, "down"), (2, "x"), (1, "down"), (2, "up"), (3, "down"), (2, "up2"), (7, "down"), (6, "x"), (1, "down2"), (8, "up"), (11, "down2"), (8, "x"), (11, "down")),
+    ((0, "x"), (0, "up"), (0, "down"), (2, "x"), (3, "x"), (2, "up"), (0, "down2"), (6, "up"), (7, "down"), (4, "up"), (7, "x"), (9, "down"), (12, "x"), (8, "x"), (9, "x")),
+    ((0, "x"), (0, "up"), (0, "down"), (1, "up"), (3, "x"), (2, "up"), (3, "down"), (6, "up"), (7, "down"), (6, "x"), (7, "x"), (7, "down2"), (12, "x"), (4, "up2"), (11, "down")),
 )
 reduce_trees = (
-    ((0, "x"), (0, "up"), (0, "down"), (2, "x"), (3, "x"), (2, "up"), (3, "down"), (6, "up"), (7, "down"), (6, "x"), (5, "down"), (8, "up"), (10, "up2"), (8, "x"), (11, "down")),
-    ((0, "x"), (0, "up"), (0, "down"), (2, "x"), (1, "down"), (2, "up"), (0, "down2"), (6, "up"), (7, "down"), (6, "x"), (7, "x"), (9, "down"), (15, "down"), (10, "up"), (9, "x")),
-    ((0, "x"), (0, "up"), (0, "down"), (2, "x"), (3, "x"), (2, "up"), (3, "down"), (6, "up"), (7, "down"), (4, "up"), (7, "x"), (7, "down2"), (12, "x"), (10, "up"), (11, "down")),
-    ((0, "x"), (0, "up"), (0, "down"), (1, "up"), (1, "down"), (0, "up2"), (0, "down2"), (6, "up"), (7, "down"), (6, "x"), (5, "down"), (6, "up2"), (14, "up"), (8, "x"), (11, "down")),
+    ((0, "x"), (0, "up"), (0, "down"), (2, "x"), (1, "down"), (2, "up"), (3, "down"), (6, "up"), (3, "down2"), (6, "x"), (5, "down"), (6, "up2"), (15, "down"), (8, "x"), (5, "down2")),
+    ((0, "x"), (0, "up"), (0, "down"), (2, "x"), (3, "x"), (2, "up"), (3, "down"), (6, "up"), (3, "down2"), (6, "x"), (5, "down"), (9, "down"), (12, "x"), (10, "up"), (9, "x")),
+    ((0, "x"), (0, "up"), (0, "down"), (2, "x"), (1, "down"), (0, "up2"), (0, "down2"), (6, "up"), (7, "down"), (6, "x"), (7, "x"), (9, "down"), (10, "up2"), (8, "x"), (9, "x")),
+    ((0, "x"), (0, "up"), (0, "down"), (1, "up"), (1, "down"), (2, "up"), (3, "down"), (6, "up"), (7, "down"), (4, "up"), (7, "x"), (9, "down"), (10, "up2"), (10, "up"), (9, "x")),
 )
 groups = (
-    ((14, 15, 9, 13), (8, 11, 2, 4), (10, 7, 12, 6), (1, 5, 3, 0)),
-    ((13, 14, 9, 7), (3, 1, 0, 2), (5, 11, 6, 4), (8, 12, 15, 10)),
-    ((12, 8, 10, 11), (9, 14, 13, 15), (0, 6, 5, 4), (1, 3, 2, 7)),
-    ((13, 10, 8, 5), (3, 15, 1, 7), (6, 14, 11, 12), (4, 2, 0, 9)),
+    ((6, 3, 0, 2), (1, 4, 13, 8), (11, 12, 15, 14), (10, 7, 9, 5)),
+    ((1, 6, 2, 5), (4, 9, 0, 3), (10, 15, 12, 8), (14, 13, 7, 11)),
+    ((8, 7, 4, 1), (2, 9, 11, 10), (3, 5, 6, 0), (13, 12, 15, 14)),
+    ((5, 14, 7, 10), (12, 8, 9, 0), (15, 13, 3, 11), (6, 1, 2, 4)),
 )
-tile_order = ((1, 1), (0, 3), (0, 2), (3, 3), (0, 1), (3, 1), (0, 0), (3, 0), (1, 0), (2, 1), (3, 2), (1, 3), (2, 0), (2, 2), (1, 2), (2, 3))
+tile_order = ((0, 0), (3, 3), (0, 3), (2, 2), (3, 1), (3, 0), (0, 2), (3, 2), (1, 3), (0, 1), (2, 3), (1, 2), (2, 0), (2, 1), (1, 1), (1, 0))
 send_rank = (
-    (3, 2, 3, 1, 3, 5, 1, 2, 4, 0, 0, 4, 0, 4, 4, 5),
-    (5, 3, 3, 2, 0, 2, 1, 1, 4, 5, 5, 5, 1, 4, 0, 1),
-    (2, 0, 5, 0, 3, 1, 2, 3, 5, 2, 1, 4, 2, 2, 0, 2),
-    (0, 4, 5, 1, 3, 3, 1, 4, 2, 1, 5, 1, 3, 2, 5, 5),
+    (4, 5, 4, 5, 0, 3, 1, 0, 0, 4, 1, 3, 1, 2, 5, 0),
+    (1, 3, 1, 1, 1, 4, 3, 4, 1, 0, 1, 3, 3, 2, 3, 5),
+    (4, 5, 2, 1, 5, 3, 2, 1, 1, 4, 3, 2, 0, 4, 4, 0),
+    (4, 4, 2, 1, 1, 2, 2, 2, 3, 5, 1, 3, 0, 4, 4, 4),
 )
 plan = {
-    "keys": [("f", 0, 0), ("f", 1, 0), ("f", 3, 0), ("f", 2, 0)],
+    "keys": [("f", 3, 0), ("f", 0, 0), ("f", 2, 0)],
     "values": [],
-    "first": [("f", 0, 3), ("f", 0, 1), ("f", 1, 3), ("f", 0, 6), ("f", 3, 3), ("f", 2, 3), ("f", 1, 2), ("w", 1, 1)],
-    0: [("f", 3, 2), ("f", 0, 7), ("f", 0, 5)],
-    1: [("r", 1, 3), ("f", 2, 2), ("f", 1, 7), ("f", 0, 10), ("f", 3, 9), ("f", 0, 12)],
-    2: [("f", 1, 4), ("f", 3, 7), ("f", 2, 7), ("r", 0, 1), ("f", 1, 6), ("f", 2, 5), ("f", 0, 9), ("w", 3, 4)],
-    3: [("f", 1, 11), ("f", 3, 6), ("f", 3, 12), ("f", 1, 9), ("f", 2, 4), ("r", 0, 12), ("f", 2, 6), ("w", 0, 8), ("w", 0, 11), ("w", 0, 2), ("w", 0, 4)],
-    4: [("r", 3, 4), ("f", 2, 9), ("r", 3, 9), ("r", 3, 2), ("w", 3, 15), ("w", 3, 1)],
-    5: [("f", 2, 12), ("r", 0, 4), ("w", 0, 14), ("w", 0, 15), ("w", 0, 13)],
-    6: [("r", 3, 15), ("r", 3, 3), ("f", 3, 8), ("w", 3, 13), ("w", 3, 10), ("w", 3, 5)],
-    7: [("r", 0, 14), ("r", 0, 15), ("r", 0, 13), ("r", 0, 9), ("w", 1, 13), ("w", 1, 14)],
-    8: [("r", 3, 13), ("r", 3, 10), ("r", 3, 7), ("w", 2, 14), ("w", 2, 13), ("w", 2, 15)],
-    9: [("r", 1, 13), ("r", 1, 14), ("w", 3, 14), ("w", 3, 11)],
-    10: [("r", 0, 8), ("r", 0, 10), ("r", 2, 9), ("r", 2, 14), ("r", 2, 15), ("r", 0, 11), ("r", 2, 13), ("r", 0, 7), ("w", 1, 8), ("w", 1, 12), ("w", 1, 15), ("w", 1, 10)],
-    11: [("r", 3, 14), ("r", 3, 11), ("r", 3, 12), ("w", 2, 8), ("w", 2, 10), ("w", 2, 11)],
-    12: [("r", 1, 8), ("r", 1, 10), ("r", 1, 15), ("r", 1, 12)],
-    13: [("r", 2, 10), ("r", 2, 11), ("r", 0, 6), ("r", 2, 8), ("r", 2, 12), ("w", 1, 5)],
-    14: [("r", 0, 5), ("r", 2, 5), ("r", 3, 8), ("w", 2, 1)],
-    15: [("r", 1, 9), ("r", 3, 5), ("r", 1, 6), ("r", 1, 11), ("r", 1, 4), ("r", 1, 5)],
-    "last": [("r", 2, 4), ("r", 2, 1), ("r", 0, 2), ("r", 2, 7), ("r", 0, 3), ("r", 2, 6), ("r", 3, 6), ("r", 1, 7), ("r", 3, 1), ("r", 1, 2), ("r", 1, 1), ("r", 2, 2), ("r", 2, 3), ("r", 0, 0), ("r", 3, 0), ("r", 1, 0), ("r", 2, 0)],
+    "first": [("f", 3, 3), ("f", 3, 2), ("f", 3, 1), ("f", 0, 3), ("f", 0, 1), ("f", 2, 3), ("f", 0, 6), ("w", 0, 2)],
+    0: [("f", 1, 0), ("f", 2, 2), ("f", 2, 7), ("f", 3, 7), ("f", 3, 6), ("f", 0, 7), ("f", 3, 4)],
+    1: [("f", 0, 9), ("f", 1, 1), ("f", 1, 3), ("f", 1, 2), ("f", 0, 8), ("w", 0, 10), ("w", 0, 5)],
+    2: [("f", 2, 6), ("f", 2, 4), ("f", 2, 9), ("w", 2, 5)],
+    3: [("r", 0, 9), ("r", 0, 7), ("f", 3, 12), ("r", 0, 10), ("f", 3, 11), ("w", 3, 8), ("w", 3, 9)],
+    4: [("r", 2, 3), ("f", 1, 11), ("r", 2, 5), ("f", 1, 8), ("w", 3, 5), ("w", 3, 14), ("w", 3, 10)],
+    5: [("f", 1, 6), ("f", 1, 7), ("f", 0, 12), ("r", 3, 8), ("r", 3, 12), ("w", 0, 11), ("w", 0, 15), ("w", 0, 14)],
+    6: [("r", 3, 14), ("r", 3, 5), ("f", 2, 8), ("f", 2, 12), ("w", 3, 15), ("w", 3, 13)],
+    7: [("r", 0, 11), ("r", 0, 14), ("r", 0, 12), ("w", 1, 14), ("w", 1, 13)],
+    8: [("r", 0, 3), ("r", 3, 13), ("r", 3, 15), ("r", 3, 11), ("w", 0, 4), ("w", 0, 13)],
+    9: [("r", 1, 13), ("r", 1, 14), ("r", 1, 7), ("r", 3, 6), ("r", 1, 11), ("w", 2, 13), ("w", 2, 15), ("w", 2, 14)],
+    10: [("r", 0, 13), ("r", 0, 8), ("r", 0, 4), ("w", 1, 10), ("w", 1, 15), ("w", 1, 12)],
+    11: [("r", 2, 13), ("r", 3, 9), ("r", 2, 12), ("r", 2, 15), ("r", 2, 14), ("w", 2, 1)],
+    12: [("r", 1, 15), ("r", 3, 10), ("r", 1, 12), ("r", 1, 8), ("r", 1, 10), ("w", 2, 11), ("w", 2, 10)],
+    13: [("r", 0, 15), ("r", 2, 1), ("r", 0, 6), ("r", 3, 2), ("r", 2, 4), ("w", 1, 4), ("w", 1, 9)],
+    14: [("r", 3, 7), ("r", 2, 8), ("r", 2, 10), ("r", 2, 11), ("r", 2, 9), ("w", 1, 5)],
+    15: [("r", 1, 4), ("r", 3, 4), ("r", 1, 9)],
+    "last": [("r", 1, 6), ("r", 1, 5), ("r", 1, 1), ("r", 0, 2), ("r", 0, 5), ("r", 2, 2), ("r", 3, 3), ("r", 2, 6), ("r", 2, 7), ("r", 3, 1), ("r", 1, 2), ("r", 1, 3), ("r", 0, 1), ("r", 3, 0), ("r", 2, 0), ("r", 1, 0), ("r", 0, 0)],
 }
-split_steps = ("first", 3)
+split_steps = ("first", 1)
 
 
 def edge(tree, slot):
@@ -238,12 +238,13 @@
             total = None
         for j in range(chunks):
             where = pl.ds(j * chunk, chunk)
-            if following is not None:
-                s = lax.dot_general(kp[key_at, where, :], q, (((1,), (1,)), ((), ())), preferred_element_type=f32) * scaling
-                if j < 2:
-                    index = lax.broadcasted_iota(jnp.int32, (chunk, 1), 0) + j * chunk
+            if following is not None and j % 2 == 0:
+                both = pl.ds(j * chunk, 2 * chunk)
+                s = lax.dot_general(kp[key_at, both, :], q, (((1,), (1,)), ((), ())), preferred_element_type=f32) * scaling
+                if j == 0:
+                    index = lax.broadcasted_iota(jnp.int32, (2 * chunk, 1), 0)
                     s = jnp.where(index <= limit, s, masked_score)
-                s_next[where, :] = s
+                s_next[both, :] = s
                 high = jnp.max(s, axis=0, keepdims=True)
                 top = high if top is None else jnp.maximum(top, high)
             if current is not None:

time: 51.3 us -> 50.9 us (level)
  no operation moved by 1% of the time
where the time goes in v5:
time: 50.9 us; the launch traced here: 50.8 us
  Pallas kernels  49.3 us (97%)
  local copies, waits for them, and re-layouts  1.57 us (3%)
    pallas_call x1, Pallas kernels, shards(): pl.pallas_call(functools.partial(kernel, (n_z, span, tokens, group_size,...  49.3 us
    unnamed x1, local copies, waits for them, and re-layouts  1.57 us

profile of v5, /device:TPU:8, one launch (start us, length us, event | category | flops | bytes accessed | tf_op | source)
XLA Modules:
  0.0 50.8 jit_solution(9596050185630807159)
XLA Ops:
  0.0 49.3 %shard_map.55 = bf16[2,16,2048]{2,1,0:T(8,128)(2,1)} custom-call(bf16[2,16,2048]{2,1,0:T(8,128)(2,1)} %q_hbm.1, s32[2]{0:T(128)} %lengths_ref.1, s32[2,16]{1,0:T(2,128)} %order_ref.1, bf16[2,4096,128]{2,1,0:T(8,128)(2,1)} %bitcast.2, bf16[2,4096,128]{2,1,0:T(8,128)(2,1)} %bitcast.3), custom_call_target="tpu_custom_call" | custom-call | tf_op jit(solution)/shard_map/pallas_call | solution.py:378
  49.3 1.6 %copy.7 = bf16[2,16,2048]{2,1,0:T(8,128)(2,1)} copy(bf16[2,16,2048]{2,1,0:T(8,128)(2,1)} %shard_map.55) | data formatting | bytes 262144
